TPU v7x, 32 devices: a whole 2x2x4 slice. The times are simulated.
32 devices in a mesh: dp: 4 (over z), expert: 8 (over y, x, core).
Axes of the slice: x: 2, y: 2, z: 4, core: 2. Of those that a mesh axis runs over, the one named last changes fastest.
Arguments:
- hidden: bfloat16 [32768, 768], P(('dp', 'expert')), may hold values from -6 to 6
- grad_out: bfloat16 [32768, 2048], P(('dp', 'expert')), may hold values from -0.19921875 to 0.19921875
- block_slot: int32 [32, 8], P(('dp', 'expert')), may hold values from 0 to 2, as said below
- block_count: int32 [32], P(('dp', 'expert')), may hold values from 2 to 8, as said below
- replica_expert: int32 [8], replicated, may hold values from 0 to 15, as said below
Outputs:
- grad_down: bfloat16 [16, 768, 2048], P('expert', None, 'dp')
Inputs may be any that keep to these rules, and one draw needn't show every extreme that they name: `replica_expert`: Expert-axis index k is home to experts k * 2 to k * 2 + 1 and has one replica slot. The indices holding an expert homed at h are h alone, or h and (h + 4) mod 8, or h and (h + m * 2) mod 8 for m = 1, 2, 3; in every draw some expert homed at index 7 has such a set of four. `block_count`: some device has all 8 blocks live. `block_slot`: block 0 of every device belongs to the replica slot 2.
All inputs are finite; a program needn't handle non-finite values.
Results may differ from a plain program's by a relative error of at most 0.0065.
Values may be sent and summed in bfloat16 or wider, within the bound.
No kernel may reach another device: no remote copies, remote signals or barrier semaphores. Data moves between devices by JAX's collectives and lax.ppermute only.
A program may use at most 128 MiB of HBM per device.

v0:
```python
import functools

import jax
import jax.numpy as jnp
from jax import lax
from jax.experimental import pallas as pl
from jax.experimental.pallas import tpu as pltpu
from jax.sharding import PartitionSpec as P

EXP_DEV = 2
ORDER = ("c3,r3", "c2,c10", "r2,r1,r0", "s3", "ma", "h3,h2,h10", "s2", "g3", "mb", "xc", "g2", "s1", "mx", "s0", "my@mb", "xh", "f", "g0")
COLD, HOT, REPLICA = 0, 1, 2
SMEM = pl.BlockSpec(memory_space=pltpu.SMEM)
VMEM = pl.BlockSpec(memory_space=pltpu.VMEM)
HBM = pl.BlockSpec(memory_space=pltpu.HBM)
ANY = pl.BlockSpec(memory_space=pl.ANY)


def params(mib):
    return pltpu.CompilerParams(vmem_limit_bytes=mib << 20)


def flip_of(k, quarter, phase):
    return 1 + (k % quarter + phase) % 2


def partner(k, quarter, flip):
    return jnp.bitwise_xor(k // quarter, flip) * quarter + k % quarter


F_HOT, F_GOES, F_PASSES, F_ARRIVES, F_BLOCKS, F_COUNT = 0, 1, 2, 3, 4, 7


def write_flags(flags, slots, counts, placement, blocks, holders):
    here = lax.axis_index("expert")
    quarter = holders // 4
    group, place = lax.rem(here, quarter), lax.div(here, quarter)

    def at(flip):
        return jnp.bitwise_xor(place, flip) * quarter + group

    def home(owner):
        return lax.div(owner, EXP_DEV)

    odd = lax.rem(group, 2)
    first, second = 1 + odd, 2 - odd
    mine, sender = placement[here], placement[at(first)]
    hot = jnp.int32(EXP_DEV - 1)
    for flip in (3, 1, 2):
        owner = placement[at(flip)]
        hot = jnp.where(home(owner) == here, lax.rem(owner, EXP_DEV), hot)
    flags[blocks + F_HOT] = hot
    flags[blocks + F_GOES] = (home(mine) == at(second)).astype(jnp.int32)
    flags[blocks + F_PASSES] = (home(sender) == at(second)).astype(jnp.int32)
    flags[blocks + F_ARRIVES] = (home(sender) == here).astype(jnp.int32)
    numbers = [jnp.int32(0)] * 3
    for b in range(blocks):
        slot = slots[0, b]
        local = jnp.where((slot == EXP_DEV) & (home(mine) == here), lax.rem(mine, EXP_DEV), slot)
        kind = jnp.where(local == EXP_DEV, REPLICA, jnp.where(local == hot, HOT, COLD))
        kind = jnp.where(b < counts[0], kind, -1)
        flags[b] = kind
        rank = jnp.int32(0)
        for i in range(3):
            rank = jnp.where(kind == i, numbers[i], rank)
            numbers[i] = numbers[i] + (kind == i).astype(jnp.int32)
        flags[blocks + F_COUNT + b] = rank
    for i in range(3):
        flags[blocks + F_BLOCKS + i] = numbers[i]


def block_copies(kind, masks, blocks, flags, hidden, grad, hidden_v, grad_v, sem, start):
    rows, width = hidden_v.shape[0] // blocks, grad_v.shape[2]

    @pl.loop(0, blocks)
    def _(b):
        @pl.when(flags[b] == kind)
        def _():
            source = pl.ds(pl.multiple_of(b * rows, rows), rows)
            target = pl.ds(pl.multiple_of(flags[blocks + F_COUNT + b] * rows, rows), rows)
            copies = [pltpu.make_async_copy(hidden.at[source, :], hidden_v.at[target, :], sem.at[0, b])]
            for j, mask in enumerate(masks):
                columns = pl.ds(pl.multiple_of(jnp.bitwise_xor(lax.axis_index("dp"), mask) * width, width), width)
                copies.append(
                    pltpu.make_async_copy(grad.at[source, columns], grad_v.at[j, target, :], sem.at[1 + j, b])
                )
            for copy in copies:
                copy.start() if start else copy.wait()


def products(kind_masks, blocks, flags, hidden, grad, scratch, outs):
    outs = list(outs)
    for (kind, masks), (hidden_v, grad_v, sem) in zip(kind_masks, scratch[2:]):
        block_copies(kind, masks, blocks, flags, hidden, grad, hidden_v, grad_v, sem, True)
    turned, total = scratch[:2]
    for (kind, masks), (hidden_v, grad_v, sem) in zip(kind_masks, scratch[2:]):
        rows = hidden_v.shape[0] // blocks
        count = flags[blocks + F_BLOCKS + kind]

        @pl.when(lax.rem(count, 2) == 1)
        def _():
            at = pl.ds(pl.multiple_of(count * rows, rows), rows)
            hidden_v[at, :] = jnp.zeros((rows, hidden_v.shape[1]), hidden_v.dtype)
            for j in range(len(masks)):
                grad_v[j, at, :] = jnp.zeros((rows, grad_v.shape[2]), grad_v.dtype)

        block_copies(kind, masks, blocks, flags, hidden, grad, hidden_v, grad_v, sem, False)

        @pl.when(count == 0)
        def _():
            for j in range(len(masks)):
                total[j] = jnp.zeros(total.shape[1:], total.dtype)

        @pl.loop(0, lax.div(count + 1, 2))
        def _(i):
            at = pl.ds(pl.multiple_of(i * 2 * rows, 2 * rows), 2 * rows)
            turned[...] = jnp.transpose(hidden_v[at, :])

            @pl.loop(0, len(masks))
            def _(j):
                def product():
                    return jnp.dot(turned[...], grad_v[j, at, :], preferred_element_type=jnp.float32)

                @pl.when(i == 0)
                def _():
                    total[j] = product()

                @pl.when(i > 0)
                def _():
                    total[j] += product()

        for j in range(len(masks)):
            outs.pop(0)[...] = total[j].astype(jnp.bfloat16)


def split_outs(groups, refs):
    pieces = []
    for group, ref in zip(groups, refs):
        pieces += [ref] if len(group) == 1 else [ref.at[i] for i in range(len(group))]
    return pieces


def by_kind(groups):
    found = []
    for group in groups:
        for kind, mask in group:
            if not found or found[-1][0] != kind:
                found.append((kind, []))
            found[-1][1].append(mask)
    return found


def opening_kernel(groups, blocks, holders, slots, counts, placement, hidden, grad, flags, *refs):
    outs = split_outs(groups, refs[: len(groups)])
    slots_s, counts_s, placement_s, small, *scratch = refs[len(groups) :]
    scalars = [
        pltpu.make_async_copy(source, target, small.at[i])
        for i, (source, target) in enumerate(((slots, slots_s), (counts, counts_s), (placement, placement_s)))
    ]
    for copy in scalars:
        copy.start()
    for copy in scalars:
        copy.wait()
    write_flags(flags, slots_s, counts_s, placement_s, blocks, holders)
    products(by_kind(groups), blocks, flags, hidden, grad, pack(scratch), outs)


def product_kernel(groups, blocks, flags, hidden, grad, *refs):
    outs = split_outs(groups, refs[1 : 1 + len(groups)])
    products(by_kind(groups), blocks, flags, hidden, grad, pack(refs[1 + len(groups) :]), outs)


def pack(scratch):
    return list(scratch[:2]) + [scratch[i : i + 3] for i in range(2, len(scratch), 3)]


def product_scratch(groups, hidden, width, blocks):
    rows, ff = hidden.shape
    found = by_kind(groups)
    most = max(len(masks) for _, masks in found)
    shapes = [pltpu.VMEM((ff, 2 * rows // blocks), hidden.dtype), pltpu.VMEM((most, ff, width), jnp.float32)]
    for _, masks in found:
        shapes += [
            pltpu.VMEM(hidden.shape, hidden.dtype),
            pltpu.VMEM((len(masks), rows, width), hidden.dtype),
            pltpu.SemaphoreType.DMA((1 + len(masks), blocks)),
        ]
    return shapes


def combine_kernel(groups, blocks, n_in, n_after, flags, *refs):
    arrays = refs[:n_in]
    outs = split_outs(groups, refs[n_in + 1 + n_after :])
    recipes = [recipe for group in groups for recipe in group]
    for out, terms in zip(outs, recipes):
        total = None
        for position, index, flag in terms:
            ref = arrays[position] if index is None else arrays[position].at[index]
            value = ref[...].astype(jnp.float32)
            if flag is not None:
                value = jnp.where(flags[blocks + flag] == 1, value, jnp.zeros_like(value))
            total = value if total is None else total + value
        out[...] = total.astype(out.dtype)


def final_kernel(recipes, blocks, n_in, flags, *refs):
    arrays, out = refs[:n_in], refs[n_in]
    buffer, sem = refs[n_in + 1 :]
    _, chunks, rows, _ = buffer.shape
    hot = flags[blocks + F_HOT]
    copies = []
    for s, terms in enumerate(recipes):
        slot = hot if s == HOT else EXP_DEV - 1 - hot
        for c in range(chunks):
            at = slice(c * rows, (c + 1) * rows)
            total = None
            for position, index in terms:
                ref = arrays[position] if index is None else arrays[position].at[index]
                value = ref[at, :].astype(jnp.float32)
                total = value if total is None else total + value
            buffer[s, c] = total.astype(buffer.dtype)
            copies.append(pltpu.make_async_copy(buffer.at[s, c], out.at[slot, pl.ds(c * rows, rows), :], sem.at[s, c]))
            copies[-1].start()
    for copy in copies:
        copy.wait()


def body(*inputs):
    n, holders = lax.axis_size("dp"), lax.axis_size("expert")
    hidden, grad, slots, counts, placement = inputs
    hidden, grad, slots, placement = (
        pltpu.with_memory_space_constraint(a, pltpu.HBM) for a in (hidden, grad, slots, placement)
    )
    (rows, ff), width, blocks = hidden.shape, grad.shape[1] // n, slots.shape[1]
    quarter = holders // 4
    chain = []
    cost = pl.CostEstimate(flops=1, bytes_accessed=1, transcendentals=0)

    def shapes_of(groups):
        lead = lambda group: () if len(group) == 1 else (len(group),)
        return [jax.ShapeDtypeStruct(lead(group) + (ff, width), jnp.bfloat16) for group in groups]

    def label(groups):
        return "_".join("chr"[group[0][0]] + "".join(str(mask) for _, mask in group) for group in groups)

    def opening(*groups):
        flags, *outs = pl.pallas_call(
            functools.partial(opening_kernel, groups, blocks, holders),
            out_shape=[jax.ShapeDtypeStruct((2 * blocks + F_COUNT,), jnp.int32)] + shapes_of(groups),
            in_specs=[HBM] * 5,
            out_specs=[SMEM] + [VMEM] * len(groups),
            scratch_shapes=[pltpu.SMEM(a.shape, a.dtype) for a in (slots, counts, placement)]
            + [pltpu.SemaphoreType.DMA((3,))]
            + product_scratch(groups, hidden, width, blocks),
            compiler_params=params(32),
            cost_estimate=cost,
            name="open_" + label(groups),
        )(slots, counts, placement, hidden, grad)
        chain.append(outs[0])
        return flags, *outs

    def product(*groups):
        outs = pl.pallas_call(
            functools.partial(product_kernel, groups, blocks),
            out_shape=shapes_of(groups),
            in_specs=[SMEM, HBM, HBM, ANY],
            out_specs=[VMEM] * len(groups),
            scratch_shapes=product_scratch(groups, hidden, width, blocks),
            compiler_params=params(32),
            cost_estimate=cost,
            name="make_" + label(groups),
        )(flags, hidden, grad, chain[-1])
        chain.append(outs[0])
        return outs

    def combine(label, arrays, *groups, after=()):
        outs = pl.pallas_call(
            functools.partial(combine_kernel, groups, blocks, len(arrays), len(after)),
            out_shape=shapes_of(groups),
            in_specs=[SMEM] + [VMEM] * len(arrays) + [ANY] * (1 + len(after)),
            out_specs=[VMEM] * len(groups),
            compiler_params=params(32),
            cost_estimate=cost,
            name="sum_" + label,
        )(flags, *arrays, chain[-1], *after)
        chain.append(outs[0])
        return outs

    def final(arrays, recipes):
        chunks = 4
        return pl.pallas_call(
            functools.partial(final_kernel, recipes, blocks, len(arrays)),
            out_shape=jax.ShapeDtypeStruct((EXP_DEV, ff, width), jnp.bfloat16),
            in_specs=[SMEM] + [VMEM] * len(arrays),
            out_specs=HBM,
            scratch_shapes=[
                pltpu.VMEM((EXP_DEV, chunks, ff // chunks, width), jnp.bfloat16),
                pltpu.SemaphoreType.DMA((EXP_DEV, chunks)),
            ],
            compiler_params=params(32),
            cost_estimate=cost,
            name="finish",
        )(flags, *arrays)

    def plane(x, phase):
        pairs = []
        for k in range(holders):
            place, group = k // quarter, k % quarter
            pairs.append((k, (place ^ (1 + (group + phase) % 2)) * quarter + group))
        return lax.ppermute(x, "expert", pairs)

    def outer(x):
        return lax.ppermute(x, "dp", [(0, 1), (n - 1, n - 2)])

    def middle(x):
        return lax.ppermute(x, "dp", [(1, 2), (2, 1)])

    def both(x):
        return lax.ppermute(x, "dp", [(0, 1), (1, 0), (2, 3), (3, 2)])

    value, at, waits = {}, {}, []
    kinds = {"c": COLD, "h": HOT, "r": REPLICA}

    def store(name, out, pieces):
        value[name] = out
        for i, piece in enumerate(pieces):
            at[piece] = (name, i if len(pieces) > 1 else None)

    def keep(names, outs):
        for name, out in zip(names, outs):
            store(name, out, [name[0] + mask for mask in name[1:]])
            if name[0] == "r":
                store("p" + name, plane(out, 0), ["p" + mask for mask in name[1:]])
            if name[0] == "c" and name[1] in "32":
                store("o" + name, outer(out), ["oc" + mask for mask in name[1:]])

    def groups_of(names):
        return [[(kinds[name[0]], int(mask)) for mask in name[1:]] for name in names]

    def sums(label, *groups):
        names, recipes = [], []
        for group in groups:
            recipes.append([])
            for terms in group:
                recipes[-1].append([])
                for piece, flag in terms:
                    name, index = at[piece]
                    if name not in names:
                        names.append(name)
                    recipes[-1][-1].append((names.index(name), index, flag))
        return combine(label, [value[name] for name in names], *recipes, after=[value[at[piece][0]] for piece in waits])

    def gathered(mask):
        return [("h" + mask, None), ("p" + mask, F_ARRIVES), ("q" + mask, None)]

    def step(name):
        nonlocal waits
        name, *waits = name.split("@")
        what, masks = name[0], name[1:]
        if what == "s":
            (out,) = sums(name, [[("r" + mask, F_GOES), ("p" + mask, F_PASSES)] for mask in masks])
            store("q" + name, plane(out, 1), ["q" + mask for mask in masks])
        elif what == "g":
            (out,) = sums(name, [gathered(mask) for mask in masks])
            store(name, out, ["g" + mask for mask in masks])
            if masks[0] in "32":
                store("o" + name, outer(out), ["oh" + mask for mask in masks])
        elif what == "m":
            own = {"a": "c2", "b": "c3", "x": "g2", "y": "g3"}
            come = {"a": "oc3", "b": "oc2", "x": "oh3", "y": "oh2"}
            (out,) = sums(name, [[(own[part], None), (come[part], None)] for part in masks])
            store("m" + name, middle(out), ["m" + part for part in masks])
        elif what == "x":
            whole = {"c": [("c1", None), ("ma", None)], "h": gathered("1") + [("mx", None)]}
            (out,) = sums(name, [whole[part] for part in masks])
            store("x" + name, both(out), ["x" + part for part in masks])
        elif what == "z":
            out, more = sums(name, [gathered("1") + [("mx", None)]], [gathered("0")])
            store("g0", more, ["g0"])
            store("x" + name, both(out), ["xh"])
        elif what == "f":
            (out,) = sums(name, [[("c0", None), ("mb", None), ("xc", None)]])
            store("f", out, ["f"])
        else:
            names = name.split(",")
            keep(names, product(*groups_of(names)))

    names = ORDER[0].split(",")
    flags, *outs = opening(*groups_of(names))
    keep(names, outs)
    for name in ORDER[1:]:
        step(name)
    lists = [["f"] if "f" in ORDER else ["c0", "mb", "xc"], ["g0", "my", "xh"]]
    names = sorted({at[piece][0] for pieces in lists for piece in pieces})
    recipe = [[(names.index(at[piece][0]), at[piece][1]) for piece in pieces] for pieces in lists]
    return final([value[name] for name in names], recipe)


def solution(mesh):
    in_specs = (
        P(("dp", "expert"), None),
        P(("dp", "expert"), None),
        P(("dp", "expert"), None),
        P(("dp", "expert")),
        P(),
    )
    out_specs = P("expert", None, "dp")
    return jax.shard_map(body, mesh=mesh, in_specs=in_specs, out_specs=out_specs, check_vma=False)
```

profile of v0, /device:TPU:8, one launch (start us, length us, event | category | flops | bytes accessed | tf_op | source)
XLA Modules:
  0.0 113.9 jit_solution(4824809357864884630)
XLA Ops:
  0.7 3.3 %open_c3_r3.1 = (s32[23]{0:T(128)S(1)}, bf16[768,512]{1,0:T(8,128)(2,1)S(1)}, bf16[768,512]{1,0:T(8,128)(2,1)S(1)}) custom-call(s32[1,8]{1,0:T(1,128)} %slots.1, s32[1]{0:T(128)S(6)} %copy.6.counts, s32[8]{0:T(128)} %placement.1, bf16[1024,768]{1,0:T(8,128)(2,1)} %hidden.7, bf16[1024,2048]{1,0:T(8,128)(2,1)} %grad.7), custom_call_target="tpu_custom_call" | custom-call | flops 1 | bytes 1 | tf_op jit(solution)/shard_map/open_c3_r3/pallas_call | solution.py:247
  4.0 3.0 %collective-permute-start.2 = (bf16[768,512]{1,0:T(8,128)(2,1)S(1)}, bf16[768,512]{1,0:T(8,128)(2,1)S(1)}, u32[]{:S(2)}, u32[]{:S(2)}) collective-permute-start(bf16[768,512]{1,0:T(8,128)(2,1)S(1)} %get-tuple-element.20.refs_0_), channel_id=1, source_target_pairs={{0,2},{1,5},{2,0},{3,7},{4,6},{5,1},{6,4},{7,3},{8,10},{9,13},{10,... | collective-permute-start | bytes 2359304 | tf_op jit(solution)/shard_map/ppermute | solution.py:310
  7.0 1.3 %collective-permute-start.1 = (bf16[768,512]{1,0:T(8,128)(2,1)S(1)}, bf16[768,512]{1,0:T(8,128)(2,1)S(1)}, u32[]{:S(2)}, u32[]{:S(2)}) collective-permute-start(bf16[768,512]{1,0:T(8,128)(2,1)S(1)} %get-tuple-element.17.refs_0_), channel_id=1, source_target_pairs={{0,8},{24,16},{1,9},{25,17},{2,10},{26,18},{3,11},{27,19},{4,12},{... | collective-permute-start | bytes 2359304 | tf_op jit(solution)/shard_map/ppermute | solution.py:313
  8.2 1.7 %make_c2_c10.1 = (bf16[768,512]{1,0:T(8,128)(2,1)S(1)}, bf16[2,768,512]{2,1,0:T(8,128)(2,1)S(1)}) custom-call(s32[23]{0:T(128)S(1)} %get-tuple-element.16.flags, bf16[1024,768]{1,0:T(8,128)(2,1)} %hidden.7, bf16[1024,2048]{1,0:T(8,128)(2,1)} %grad.7, bf16[768,512]{1,0:T(8,128)(2,1)S(1)} %get-tuple-element.17.refs_0_), custom_call_target="tpu_custom_call" | custom-call | flops 1 | bytes 1 | tf_op jit(solution)/shard_map/make_c2_c10/pallas_call | solution.py:263
  10.0 3.5 %make_r2_r1_r0.1 = (bf16[768,512]{1,0:T(8,128)(2,1)S(1)}, bf16[768,512]{1,0:T(8,128)(2,1)S(1)}, bf16[768,512]{1,0:T(8,128)(2,1)S(1)}) custom-call(s32[23]{0:T(128)S(1)} %get-tuple-element.16.flags, bf16[1024,768]{1,0:T(8,128)(2,1)} %hidden.7, bf16[1024,2048]{1,0:T(8,128)(2,1)} %grad.7, bf16[768,512]{1,0:T(8,128)(2,1)S(1)} %get-tuple-element.19.refs_0_), custom_call_target="tpu_custom_call" | custom-call | flops 1 | bytes 1 | tf_op jit(solution)/shard_map/make_r2_r1_r0/pallas_call | solution.py:263
  13.4 3.8 %collective-permute-start.4 = (bf16[768,512]{1,0:T(8,128)(2,1)S(1)}, bf16[768,512]{1,0:T(8,128)(2,1)S(1)}, u32[]{:S(2)}, u32[]{:S(2)}) collective-permute-start(bf16[768,512]{1,0:T(8,128)(2,1)S(1)} %get-tuple-element.21.refs_2_.refs_0_), channel_id=1, source_target_pairs={{0,2},{1,5},{2,0},{3,7},{4,6},{5,1},{6,4},{7,3},{8,10},{9,13},{10,... | collective-permute-start | bytes 2359304 | tf_op jit(solution)/shard_map/ppermute | solution.py:310
  17.3 0.8 sum_s3.1.refs_2_
  18.1 1.5 %collective-permute-start.3 = (bf16[768,512]{1,0:T(8,128)(2,1)S(1)}, bf16[768,512]{1,0:T(8,128)(2,1)S(1)}, u32[]{:S(2)}, u32[]{:S(2)}) collective-permute-start(bf16[768,512]{1,0:T(8,128)(2,1)S(1)} %sum_s3.1.refs_2_), channel_id=1, source_target_pairs={{0,4},{1,3},{2,6},{3,1},{4,0},{5,7},{6,2},{7,5},{8,12},{9,11},{10,... | collective-permute-start | bytes 2359304 | tf_op jit(solution)/shard_map/ppermute | solution.py:310
  19.6 1.3 %collective-permute-start = (bf16[768,512]{1,0:T(8,128)(2,1)S(1)}, bf16[768,512]{1,0:T(8,128)(2,1)S(1)}, u32[]{:S(2)}, u32[]{:S(2)}) collective-permute-start(bf16[768,512]{1,0:T(8,128)(2,1)S(1)} %get-tuple-element.19.refs_0_), channel_id=1, source_target_pairs={{0,8},{24,16},{1,9},{25,17},{2,10},{26,18},{3,11},{27,19},{4,12},{... | collective-permute-start | bytes 2359304 | tf_op jit(solution)/shard_map/ppermute | solution.py:313
  20.9 8.4 %collective-permute-done.1.refs_1_ = bf16[768,512]{1,0:T(8,128)(2,1)S(1)} collective-permute-done((bf16[768,512]{1,0:T(8,128)(2,1)S(1)}, bf16[768,512]{1,0:T(8,128)(2,1)S(1)}, u32[]{:S(2)}, u32[]{:S(2)}) %collective-permute-start.1) | collective-permute-done | bytes 786464 | tf_op jit(solution)/shard_map/ppermute | solution.py:313
  29.3 0.7 sum_ma.1.refs_0_
  30.0 2.8 %collective-permute-start.6 = (bf16[768,512]{1,0:T(8,128)(2,1)S(1)}, bf16[768,512]{1,0:T(8,128)(2,1)S(1)}, u32[]{:S(2)}, u32[]{:S(2)}) collective-permute-start(bf16[768,512]{1,0:T(8,128)(2,1)S(1)} %sum_ma.1.refs_0_), channel_id=1, source_target_pairs={{8,16},{16,8},{9,17},{17,9},{10,18},{18,10},{11,19},{19,11},{12,20... | collective-permute-start | bytes 2359304 | tf_op jit(solution)/shard_map/ppermute | solution.py:316
  32.8 4.1 %make_h3_h2_h10.1 = (bf16[768,512]{1,0:T(8,128)(2,1)S(1)}, bf16[768,512]{1,0:T(8,128)(2,1)S(1)}, bf16[2,768,512]{2,1,0:T(8,128)(2,1)S(1)}) custom-call(s32[23]{0:T(128)S(1)} %get-tuple-element.16.flags, bf16[1024,768]{1,0:T(8,128)(2,1)} %hidden.7, bf16[1024,2048]{1,0:T(8,128)(2,1)} %grad.7, bf16[768,512]{1,0:T(8,128)(2,1)S(1)} %sum_ma.1.refs_0_), custom_call_target="tpu_custom_call" | custom-call | flops 1 | bytes 1 | tf_op jit(solution)/shard_map/make_h3_h2_h10/pallas_call | solution.py:263
  36.9 0.0 collective-permute-done.4.refs_1_
  36.9 0.8 sum_s2.1.refs_3_
  37.8 1.1 collective-permute-start.9
  38.9 1.2 %collective-permute-start.8 = (bf16[768,512]{1,0:T(8,128)(2,1)S(1)}, bf16[768,512]{1,0:T(8,128)(2,1)S(1)}, u32[]{:S(2)}, u32[]{:S(2)}) collective-permute-start(bf16[768,512]{1,0:T(8,128)(2,1)S(1)} %get-tuple-element.24.refs_0_), channel_id=1, source_target_pairs={{0,2},{1,5},{2,0},{3,7},{4,6},{5,1},{6,4},{7,3},{8,10},{9,13},{10,... | collective-permute-start | bytes 2359304 | tf_op jit(solution)/shard_map/ppermute | solution.py:310
  40.1 0.9 sum_g3.1.refs_2_.refs_0_
  41.0 1.3 %collective-permute-start.11 = (bf16[768,512]{1,0:T(8,128)(2,1)S(1)}, bf16[768,512]{1,0:T(8,128)(2,1)S(1)}, u32[]{:S(2)}, u32[]{:S(2)}) collective-permute-start(bf16[768,512]{1,0:T(8,128)(2,1)S(1)} %sum_g3.1.refs_2_.refs_0_), channel_id=1, source_target_pairs={{0,8},{24,16},{1,9},{25,17},{2,10},{26,18},{3,11},{27,19},{4,12},{... | collective-permute-start | bytes 2359304 | tf_op jit(solution)/shard_map/ppermute | solution.py:313
  42.3 2.8 %collective-permute-done.refs_1_ = bf16[768,512]{1,0:T(8,128)(2,1)S(1)} collective-permute-done((bf16[768,512]{1,0:T(8,128)(2,1)S(1)}, bf16[768,512]{1,0:T(8,128)(2,1)S(1)}, u32[]{:S(2)}, u32[]{:S(2)}) %collective-permute-start) | collective-permute-done | bytes 786464 | tf_op jit(solution)/shard_map/ppermute | solution.py:313
  45.1 0.2 collective-permute-start.14
  45.3 0.7 sum_mb.1.refs_2_
  46.0 3.1 %collective-permute-done.6.refs_1_ = bf16[768,512]{1,0:T(8,128)(2,1)S(1)} collective-permute-done((bf16[768,512]{1,0:T(8,128)(2,1)S(1)}, bf16[768,512]{1,0:T(8,128)(2,1)S(1)}, u32[]{:S(2)}, u32[]{:S(2)}) %collective-permute-start.6) | collective-permute-done | bytes 786464 | tf_op jit(solution)/shard_map/ppermute | solution.py:316
  49.1 3.6 %collective-permute-start.5 = (bf16[768,512]{1,0:T(8,128)(2,1)S(1)}, bf16[768,512]{1,0:T(8,128)(2,1)S(1)}, u32[]{:S(2)}, u32[]{:S(2)}) collective-permute-start(bf16[768,512]{1,0:T(8,128)(2,1)S(1)} %sum_mb.1.refs_2_), channel_id=1, source_target_pairs={{8,16},{16,8},{9,17},{17,9},{10,18},{18,10},{11,19},{19,11},{12,20... | collective-permute-start | bytes 2359304 | tf_op jit(solution)/shard_map/ppermute | solution.py:316
  52.8 0.7 sum_xc.1.refs_3_
  53.5 4.7 %collective-permute-done.9.refs_2_ = bf16[768,512]{1,0:T(8,128)(2,1)S(1)} collective-permute-done((bf16[768,512]{1,0:T(8,128)(2,1)S(1)}, bf16[768,512]{1,0:T(8,128)(2,1)S(1)}, u32[]{:S(2)}, u32[]{:S(2)}) %collective-permute-start.9) | collective-permute-done | bytes 786464 | tf_op jit(solution)/shard_map/ppermute | solution.py:310
  58.2 0.9 sum_g2.1.refs_2_.refs_0_
  59.1 1.3 %collective-permute-start.13 = (bf16[768,512]{1,0:T(8,128)(2,1)S(1)}, bf16[768,512]{1,0:T(8,128)(2,1)S(1)}, u32[]{:S(2)}, u32[]{:S(2)}) collective-permute-start(bf16[768,512]{1,0:T(8,128)(2,1)S(1)} %sum_g2.1.refs_2_.refs_0_), channel_id=1, source_target_pairs={{0,8},{24,16},{1,9},{25,17},{2,10},{26,18},{3,11},{27,19},{4,12},{... | collective-permute-start | bytes 2359304 | tf_op jit(solution)/shard_map/ppermute | solution.py:313
  60.4 0.8 sum_s1.1.refs_2_
  61.3 1.1 collective-permute-start.10
  62.3 3.1 %collective-permute-done.11.refs_1_ = bf16[768,512]{1,0:T(8,128)(2,1)S(1)} collective-permute-done((bf16[768,512]{1,0:T(8,128)(2,1)S(1)}, bf16[768,512]{1,0:T(8,128)(2,1)S(1)}, u32[]{:S(2)}, u32[]{:S(2)}) %collective-permute-start.11) | collective-permute-done | bytes 786464 | tf_op jit(solution)/shard_map/ppermute | solution.py:313
  65.5 0.7 sum_mx.1.refs_2_
  66.2 1.9 %collective-permute-start.12 = (bf16[768,512]{1,0:T(8,128)(2,1)S(1)}, bf16[768,512]{1,0:T(8,128)(2,1)S(1)}, u32[]{:S(2)}, u32[]{:S(2)}) collective-permute-start(bf16[768,512]{1,0:T(8,128)(2,1)S(1)} %sum_mx.1.refs_2_), channel_id=1, source_target_pairs={{8,16},{16,8},{9,17},{17,9},{10,18},{18,10},{11,19},{19,11},{12,20... | collective-permute-start | bytes 2359304 | tf_op jit(solution)/shard_map/ppermute | solution.py:316
  68.1 0.6 collective-permute-done.14.refs_1_
  68.7 0.8 sum_s0.1.refs_2_
  69.5 1.8 %collective-permute-done.5.refs_3_.refs_1_ = bf16[768,512]{1,0:T(8,128)(2,1)S(1)} collective-permute-done((bf16[768,512]{1,0:T(8,128)(2,1)S(1)}, bf16[768,512]{1,0:T(8,128)(2,1)S(1)}, u32[]{:S(2)}, u32[]{:S(2)}) %collective-permute-start.5) | collective-permute-done | bytes 786464 | tf_op jit(solution)/shard_map/ppermute | solution.py:316
  71.3 11.0 %collective-permute-done.13.refs_1_ = bf16[768,512]{1,0:T(8,128)(2,1)S(1)} collective-permute-done((bf16[768,512]{1,0:T(8,128)(2,1)S(1)}, bf16[768,512]{1,0:T(8,128)(2,1)S(1)}, u32[]{:S(2)}, u32[]{:S(2)}) %collective-permute-start.13) | collective-permute-done | bytes 786464 | tf_op jit(solution)/shard_map/ppermute | solution.py:313
  82.3 0.7 sum_my.1.refs_4_
  83.0 2.2 %collective-permute-start.16 = (bf16[768,512]{1,0:T(8,128)(2,1)S(1)}, bf16[768,512]{1,0:T(8,128)(2,1)S(1)}, u32[]{:S(2)}, u32[]{:S(2)}) collective-permute-start(bf16[768,512]{1,0:T(8,128)(2,1)S(1)} %sum_my.1.refs_4_), channel_id=1, source_target_pairs={{8,16},{16,8},{9,17},{17,9},{10,18},{18,10},{11,19},{19,11},{12,20... | collective-permute-start | bytes 2359304 | tf_op jit(solution)/shard_map/ppermute | solution.py:316
  85.3 3.3 %collective-permute-done.12.refs_3_ = bf16[768,512]{1,0:T(8,128)(2,1)S(1)} collective-permute-done((bf16[768,512]{1,0:T(8,128)(2,1)S(1)}, bf16[768,512]{1,0:T(8,128)(2,1)S(1)}, u32[]{:S(2)}, u32[]{:S(2)}) %collective-permute-start.12) | collective-permute-done | bytes 786464 | tf_op jit(solution)/shard_map/ppermute | solution.py:316
  88.6 1.0 sum_xh.1.refs_3_
  89.5 0.1 collective-permute-start.17
  89.6 9.5 %collective-permute-done.7.refs_2_ = bf16[768,512]{1,0:T(8,128)(2,1)S(1)} collective-permute-done((bf16[768,512]{1,0:T(8,128)(2,1)S(1)}, bf16[768,512]{1,0:T(8,128)(2,1)S(1)}, u32[]{:S(2)}, u32[]{:S(2)}) %collective-permute-start.7) | collective-permute-done | bytes 786464 | tf_op jit(solution)/shard_map/ppermute | solution.py:319
  99.2 0.8 sum_f.1.refs_3_.refs_0_
  100.0 0.9 sum_g0.1.refs_1_
  100.9 1.0 collective-permute-done.16.refs_2_
  101.9 10.2 %collective-permute-done.17.refs_3_ = bf16[768,512]{1,0:T(8,128)(2,1)S(1)} collective-permute-done((bf16[768,512]{1,0:T(8,128)(2,1)S(1)}, bf16[768,512]{1,0:T(8,128)(2,1)S(1)}, u32[]{:S(2)}, u32[]{:S(2)}) %collective-permute-start.17) | collective-permute-done | bytes 786464 | tf_op jit(solution)/shard_map/ppermute | solution.py:319
  112.1 1.7 %finish.1 = bf16[2,768,512]{2,1,0:T(8,128)(2,1)} custom-call(s32[23]{0:T(128)S(1)} %get-tuple-element.16.flags, bf16[768,512]{1,0:T(8,128)(2,1)S(1)} %sum_f.1.refs_3_.refs_0_, bf16[768,512]{1,0:T(8,128)(2,1)S(1)} %sum_g0.1.refs_1_, bf16[768,512]{1,0:T(8,128)(2,1)S(1)} %collective-permute-done.16.refs_2_, bf16[768,512]{1,0:T(8,128)(2,1)S(1)} %collective-permute-done.17.refs_3_), custom_call_target="tpu_custom_call" | custom-call | flops 1 | bytes 1 | tf_op jit(solution)/shard_map/finish/pallas_call | solution.py:291
  (7 shorter events, 0.0 us)
Async XLA Ops:
  4.0 13.3 %collective-permute-start.2 = (bf16[768,512]{1,0:T(8,128)(2,1)S(1)}, bf16[768,512]{1,0:T(8,128)(2,1)S(1)}, u32[]{:S(2)}, u32[]{:S(2)}) collective-permute-start(bf16[768,512]{1,0:T(8,128)(2,1)S(1)} %get-tuple-element.20.refs_0_), channel_id=1, source_target_pairs={{0,2},{1,5},{2,0},{3,7},{4,6},{5,1},{6,4},{7,3},{8,10},{9,13},{10,... | collective-permute-start | bytes 2359304 | tf_op jit(solution)/shard_map/ppermute | solution.py:310
  7.0 22.4 %collective-permute-start.1 = (bf16[768,512]{1,0:T(8,128)(2,1)S(1)}, bf16[768,512]{1,0:T(8,128)(2,1)S(1)}, u32[]{:S(2)}, u32[]{:S(2)}) collective-permute-start(bf16[768,512]{1,0:T(8,128)(2,1)S(1)} %get-tuple-element.17.refs_0_), channel_id=1, source_target_pairs={{0,8},{24,16},{1,9},{25,17},{2,10},{26,18},{3,11},{27,19},{4,12},{... | collective-permute-start | bytes 2359304 | tf_op jit(solution)/shard_map/ppermute | solution.py:313
  13.4 23.5 %collective-permute-start.4 = (bf16[768,512]{1,0:T(8,128)(2,1)S(1)}, bf16[768,512]{1,0:T(8,128)(2,1)S(1)}, u32[]{:S(2)}, u32[]{:S(2)}) collective-permute-start(bf16[768,512]{1,0:T(8,128)(2,1)S(1)} %get-tuple-element.21.refs_2_.refs_0_), channel_id=1, source_target_pairs={{0,2},{1,5},{2,0},{3,7},{4,6},{5,1},{6,4},{7,3},{8,10},{9,13},{10,... | collective-permute-start | bytes 2359304 | tf_op jit(solution)/shard_map/ppermute | solution.py:310
  18.1 22.0 %collective-permute-start.3 = (bf16[768,512]{1,0:T(8,128)(2,1)S(1)}, bf16[768,512]{1,0:T(8,128)(2,1)S(1)}, u32[]{:S(2)}, u32[]{:S(2)}) collective-permute-start(bf16[768,512]{1,0:T(8,128)(2,1)S(1)} %sum_s3.1.refs_2_), channel_id=1, source_target_pairs={{0,4},{1,3},{2,6},{3,1},{4,0},{5,7},{6,2},{7,5},{8,12},{9,11},{10,... | collective-permute-start | bytes 2359304 | tf_op jit(solution)/shard_map/ppermute | solution.py:310
  19.6 25.4 %collective-permute-start = (bf16[768,512]{1,0:T(8,128)(2,1)S(1)}, bf16[768,512]{1,0:T(8,128)(2,1)S(1)}, u32[]{:S(2)}, u32[]{:S(2)}) collective-permute-start(bf16[768,512]{1,0:T(8,128)(2,1)S(1)} %get-tuple-element.19.refs_0_), channel_id=1, source_target_pairs={{0,8},{24,16},{1,9},{25,17},{2,10},{26,18},{3,11},{27,19},{4,12},{... | collective-permute-start | bytes 2359304 | tf_op jit(solution)/shard_map/ppermute | solution.py:313
  30.0 19.1 %collective-permute-start.6 = (bf16[768,512]{1,0:T(8,128)(2,1)S(1)}, bf16[768,512]{1,0:T(8,128)(2,1)S(1)}, u32[]{:S(2)}, u32[]{:S(2)}) collective-permute-start(bf16[768,512]{1,0:T(8,128)(2,1)S(1)} %sum_ma.1.refs_0_), channel_id=1, source_target_pairs={{8,16},{16,8},{9,17},{17,9},{10,18},{18,10},{11,19},{19,11},{12,20... | collective-permute-start | bytes 2359304 | tf_op jit(solution)/shard_map/ppermute | solution.py:316
  37.8 20.5 %collective-permute-start.9 = (bf16[768,512]{1,0:T(8,128)(2,1)S(1)}, bf16[768,512]{1,0:T(8,128)(2,1)S(1)}, u32[]{:S(2)}, u32[]{:S(2)}) collective-permute-start(bf16[768,512]{1,0:T(8,128)(2,1)S(1)} %sum_s2.1.refs_3_), channel_id=1, source_target_pairs={{0,4},{1,3},{2,6},{3,1},{4,0},{5,7},{6,2},{7,5},{8,12},{9,11},{10,... | collective-permute-start | bytes 2359304 | tf_op jit(solution)/shard_map/ppermute | solution.py:310
  38.9 21.5 %collective-permute-start.8 = (bf16[768,512]{1,0:T(8,128)(2,1)S(1)}, bf16[768,512]{1,0:T(8,128)(2,1)S(1)}, u32[]{:S(2)}, u32[]{:S(2)}) collective-permute-start(bf16[768,512]{1,0:T(8,128)(2,1)S(1)} %get-tuple-element.24.refs_0_), channel_id=1, source_target_pairs={{0,2},{1,5},{2,0},{3,7},{4,6},{5,1},{6,4},{7,3},{8,10},{9,13},{10,... | collective-permute-start | bytes 2359304 | tf_op jit(solution)/shard_map/ppermute | solution.py:310
  41.0 24.5 %collective-permute-start.11 = (bf16[768,512]{1,0:T(8,128)(2,1)S(1)}, bf16[768,512]{1,0:T(8,128)(2,1)S(1)}, u32[]{:S(2)}, u32[]{:S(2)}) collective-permute-start(bf16[768,512]{1,0:T(8,128)(2,1)S(1)} %sum_g3.1.refs_2_.refs_0_), channel_id=1, source_target_pairs={{0,8},{24,16},{1,9},{25,17},{2,10},{26,18},{3,11},{27,19},{4,12},{... | collective-permute-start | bytes 2359304 | tf_op jit(solution)/shard_map/ppermute | solution.py:313
  45.1 23.6 %collective-permute-start.14 = (bf16[768,512]{1,0:T(8,128)(2,1)S(1)}, bf16[768,512]{1,0:T(8,128)(2,1)S(1)}, u32[]{:S(2)}, u32[]{:S(2)}) collective-permute-start(bf16[768,512]{1,0:T(8,128)(2,1)S(1)} %get-tuple-element.26.refs_0_), channel_id=1, source_target_pairs={{0,2},{1,5},{2,0},{3,7},{4,6},{5,1},{6,4},{7,3},{8,10},{9,13},{10,... | collective-permute-start | bytes 2359304 | tf_op jit(solution)/shard_map/ppermute | solution.py:310
  49.1 22.1 %collective-permute-start.5 = (bf16[768,512]{1,0:T(8,128)(2,1)S(1)}, bf16[768,512]{1,0:T(8,128)(2,1)S(1)}, u32[]{:S(2)}, u32[]{:S(2)}) collective-permute-start(bf16[768,512]{1,0:T(8,128)(2,1)S(1)} %sum_mb.1.refs_2_), channel_id=1, source_target_pairs={{8,16},{16,8},{9,17},{17,9},{10,18},{18,10},{11,19},{19,11},{12,20... | collective-permute-start | bytes 2359304 | tf_op jit(solution)/shard_map/ppermute | solution.py:316
  59.1 23.2 %collective-permute-start.13 = (bf16[768,512]{1,0:T(8,128)(2,1)S(1)}, bf16[768,512]{1,0:T(8,128)(2,1)S(1)}, u32[]{:S(2)}, u32[]{:S(2)}) collective-permute-start(bf16[768,512]{1,0:T(8,128)(2,1)S(1)} %sum_g2.1.refs_2_.refs_0_), channel_id=1, source_target_pairs={{0,8},{24,16},{1,9},{25,17},{2,10},{26,18},{3,11},{27,19},{4,12},{... | collective-permute-start | bytes 2359304 | tf_op jit(solution)/shard_map/ppermute | solution.py:313
  61.3 24.0 %collective-permute-start.10 = (bf16[768,512]{1,0:T(8,128)(2,1)S(1)}, bf16[768,512]{1,0:T(8,128)(2,1)S(1)}, u32[]{:S(2)}, u32[]{:S(2)}) collective-permute-start(bf16[768,512]{1,0:T(8,128)(2,1)S(1)} %sum_s1.1.refs_2_), channel_id=1, source_target_pairs={{0,4},{1,3},{2,6},{3,1},{4,0},{5,7},{6,2},{7,5},{8,12},{9,11},{10,... | collective-permute-start | bytes 2359304 | tf_op jit(solution)/shard_map/ppermute | solution.py:310
  66.2 22.4 %collective-permute-start.12 = (bf16[768,512]{1,0:T(8,128)(2,1)S(1)}, bf16[768,512]{1,0:T(8,128)(2,1)S(1)}, u32[]{:S(2)}, u32[]{:S(2)}) collective-permute-start(bf16[768,512]{1,0:T(8,128)(2,1)S(1)} %sum_mx.1.refs_2_), channel_id=1, source_target_pairs={{8,16},{16,8},{9,17},{17,9},{10,18},{18,10},{11,19},{19,11},{12,20... | collective-permute-start | bytes 2359304 | tf_op jit(solution)/shard_map/ppermute | solution.py:316
  68.7 30.5 %collective-permute-start.7 = (bf16[768,512]{1,0:T(8,128)(2,1)S(1)}, bf16[768,512]{1,0:T(8,128)(2,1)S(1)}, u32[]{:S(2)}, u32[]{:S(2)}) collective-permute-start(bf16[768,512]{1,0:T(8,128)(2,1)S(1)} %sum_xc.1.refs_3_), channel_id=1, source_target_pairs={{0,8},{8,0},{16,24},{24,16},{1,9},{9,1},{17,25},{25,17},{2,10},{10... | collective-permute-start | bytes 2359304 | tf_op jit(solution)/shard_map/ppermute | solution.py:319
  71.3 28.7 %collective-permute-start.15 = (bf16[768,512]{1,0:T(8,128)(2,1)S(1)}, bf16[768,512]{1,0:T(8,128)(2,1)S(1)}, u32[]{:S(2)}, u32[]{:S(2)}) collective-permute-start(bf16[768,512]{1,0:T(8,128)(2,1)S(1)} %sum_s0.1.refs_2_), channel_id=1, source_target_pairs={{0,4},{1,3},{2,6},{3,1},{4,0},{5,7},{6,2},{7,5},{8,12},{9,11},{10,... | collective-permute-start | bytes 2359304 | tf_op jit(solution)/shard_map/ppermute | solution.py:310
  83.0 18.8 %collective-permute-start.16 = (bf16[768,512]{1,0:T(8,128)(2,1)S(1)}, bf16[768,512]{1,0:T(8,128)(2,1)S(1)}, u32[]{:S(2)}, u32[]{:S(2)}) collective-permute-start(bf16[768,512]{1,0:T(8,128)(2,1)S(1)} %sum_my.1.refs_4_), channel_id=1, source_target_pairs={{8,16},{16,8},{9,17},{17,9},{10,18},{18,10},{11,19},{19,11},{12,20... | collective-permute-start | bytes 2359304 | tf_op jit(solution)/shard_map/ppermute | solution.py:316
  89.5 22.6 %collective-permute-start.17 = (bf16[768,512]{1,0:T(8,128)(2,1)S(1)}, bf16[768,512]{1,0:T(8,128)(2,1)S(1)}, u32[]{:S(2)}, u32[]{:S(2)}) collective-permute-start(bf16[768,512]{1,0:T(8,128)(2,1)S(1)} %sum_xh.1.refs_3_), channel_id=1, source_target_pairs={{0,8},{8,0},{16,24},{24,16},{1,9},{9,1},{17,25},{25,17},{2,10},{10... | collective-permute-start | bytes 2359304 | tf_op jit(solution)/shard_map/ppermute | solution.py:319
where the time goes:
time: 114 us
  waiting for transfers between devices  59.6 us (52%)
  starting transfers between devices  27.7 us (24%)
  Pallas kernels  25.6 us (22%)
    ppermute x4, waiting for transfers between devices, outer(): return lax.ppermute(x, 'dp', [(0, 1), (n - 1, n - 2)])  25.3 us
    ppermute x2, waiting for transfers between devices, both(): return lax.ppermute(x, 'dp', [(0, 1), (1, 0), (2, 3), (3, 2)])  19.8 us
    ppermute x8, starting transfers between devices, plane(): return lax.ppermute(x, 'expert', pairs)  11.9 us
    pallas_call x14, Pallas kernels, combine(): pl.pallas_call(functools.partial(combine_kernel, groups, blocks, len(arra...  11.3 us
    ppermute x4, starting transfers between devices, middle(): return lax.ppermute(x, 'dp', [(1, 2), (2, 1)])  10.6 us
    pallas_call x3, Pallas kernels, product(): pl.pallas_call(functools.partial(product_kernel, groups, blocks), out_sha...  9.23 us
    ppermute x4, waiting for transfers between devices, middle(): return lax.ppermute(x, 'dp', [(1, 2), (2, 1)])  9.19 us
    ppermute x8, waiting for transfers between devices, plane(): return lax.ppermute(x, 'expert', pairs)  5.3 us
  transfers between devices with their start and end apart: 18, of which 12 were waited for; matrix products, arithmetic and copies ran while one was open for 0% of the time, Pallas kernels for 18%

commit v1 on v0

--- a/solution.py
+++ b/solution.py
@@ -152,17 +152,71 @@
 
 def opening_kernel(groups, blocks, holders, slots, counts, placement, hidden, grad, flags, *refs):
     outs = split_outs(groups, refs[: len(groups)])
-    slots_s, counts_s, placement_s, small, *scratch = refs[len(groups) :]
+    slots_s, counts_s, placement_s, order, turned, pair, total, hidden_v, grad_v, small, sem = refs[len(groups) :]
+    found = by_kind(groups)
+    rows, width = hidden_v.shape[0] // blocks, grad_v.shape[1]
+    begin = pl.multiple_of(jnp.bitwise_xor(lax.axis_index("dp"), found[0][1][0]) * width, width)
     scalars = [
         pltpu.make_async_copy(source, target, small.at[i])
         for i, (source, target) in enumerate(((slots, slots_s), (counts, counts_s), (placement, placement_s)))
     ]
-    for copy in scalars:
+    loads = []
+    for part in range(sem.shape[1]):
+        step = hidden_v.shape[0] // sem.shape[1]
+        at = pl.ds(part * step, step)
+        loads.append(pltpu.make_async_copy(hidden.at[at, :], hidden_v.at[at, :], sem.at[0, part]))
+        loads.append(pltpu.make_async_copy(grad.at[at, pl.ds(begin, width)], grad_v.at[at, :], sem.at[1, part]))
+    for copy in scalars + loads:
         copy.start()
     for copy in scalars:
         copy.wait()
     write_flags(flags, slots_s, counts_s, placement_s, blocks, holders)
-    products(by_kind(groups), blocks, flags, hidden, grad, pack(scratch), outs)
+    for b in range(blocks):
+        kind = flags[b]
+        order[jnp.where(kind < 0, 3, kind) * blocks + flags[blocks + F_COUNT + b]] = b
+    for copy in loads:
+        copy.wait()
+    for (kind, _), out in zip(found, outs):
+        count = flags[blocks + F_BLOCKS + kind]
+
+        @pl.when(count == 0)
+        def _(out=out):
+            out[...] = jnp.zeros(out.shape, out.dtype)
+
+        @pl.loop(0, lax.div(count + 1, 2))
+        def _(i, kind=kind, count=count):
+            for half in range(2):
+                mine = slice(half * rows, (half + 1) * rows)
+
+                def take(half=half, mine=mine):
+                    at = pl.ds(pl.multiple_of(order[kind * blocks + 2 * i + half] * rows, rows), rows)
+                    turned[:, mine] = jnp.transpose(hidden_v[at, :])
+                    pair[mine, :] = grad_v[at, :]
+
+                def clear(mine=mine):
+                    turned[:, mine] = jnp.zeros((turned.shape[0], rows), turned.dtype)
+                    pair[mine, :] = jnp.zeros((rows, width), pair.dtype)
+
+                if half == 0:
+                    take()
+                else:
+                    pl.when(2 * i + 1 < count)(take)
+                    pl.when(2 * i + 1 >= count)(clear)
+
+            def product():
+                return jnp.dot(turned[...], pair[...], preferred_element_type=jnp.float32)
+
+            @pl.when(i == 0)
+            def _():
+                total[...] = product()
+
+            @pl.when(i > 0)
+            def _():
+                total[...] += product()
+
+        @pl.when(count > 0)
+        def _(out=out):
+            out[...] = total[...].astype(out.dtype)
 
 
 def product_kernel(groups, blocks, flags, hidden, grad, *refs):
@@ -203,24 +257,22 @@
         out[...] = total.astype(out.dtype)
 
 
-def final_kernel(recipes, blocks, n_in, flags, *refs):
-    arrays, out = refs[:n_in], refs[n_in]
-    buffer, sem = refs[n_in + 1 :]
-    _, chunks, rows, _ = buffer.shape
+def place_kernel(terms, is_hot, blocks, n_in, flags, *refs):
+    arrays, (out, buffer, sem) = refs[:n_in], refs[-3:]
+    chunks, rows, _ = buffer.shape
     hot = flags[blocks + F_HOT]
+    slot = hot if is_hot else EXP_DEV - 1 - hot
     copies = []
-    for s, terms in enumerate(recipes):
-        slot = hot if s == HOT else EXP_DEV - 1 - hot
-        for c in range(chunks):
-            at = slice(c * rows, (c + 1) * rows)
-            total = None
-            for position, index in terms:
-                ref = arrays[position] if index is None else arrays[position].at[index]
-                value = ref[at, :].astype(jnp.float32)
-                total = value if total is None else total + value
-            buffer[s, c] = total.astype(buffer.dtype)
-            copies.append(pltpu.make_async_copy(buffer.at[s, c], out.at[slot, pl.ds(c * rows, rows), :], sem.at[s, c]))
-            copies[-1].start()
+    for c in range(chunks):
+        at = slice(c * rows, (c + 1) * rows)
+        total = None
+        for position, index in terms:
+            ref = arrays[position] if index is None else arrays[position].at[index]
+            value = ref[at, :].astype(jnp.float32)
+            total = value if total is None else total + value
+        buffer[c] = total.astype(buffer.dtype)
+        copies.append(pltpu.make_async_copy(buffer.at[c], out.at[slot, pl.ds(c * rows, rows), :], sem.at[c]))
+        copies[-1].start()
     for copy in copies:
         copy.wait()
 
@@ -250,8 +302,16 @@
             in_specs=[HBM] * 5,
             out_specs=[SMEM] + [VMEM] * len(groups),
             scratch_shapes=[pltpu.SMEM(a.shape, a.dtype) for a in (slots, counts, placement)]
-            + [pltpu.SemaphoreType.DMA((3,))]
-            + product_scratch(groups, hidden, width, blocks),
+            + [
+                pltpu.SMEM((4 * blocks,), jnp.int32),
+                pltpu.VMEM((ff, 2 * rows // blocks), hidden.dtype),
+                pltpu.VMEM((2 * rows // blocks, width), grad.dtype),
+                pltpu.VMEM((ff, width), jnp.float32),
+                pltpu.VMEM((rows, ff), hidden.dtype),
+                pltpu.VMEM((rows, width), grad.dtype),
+                pltpu.SemaphoreType.DMA((3,)),
+                pltpu.SemaphoreType.DMA((2, 4)),
+            ],
             compiler_params=params(32),
             cost_estimate=cost,
             name="open_" + label(groups),
@@ -286,21 +346,28 @@
         chain.append(outs[0])
         return outs
 
-    def final(arrays, recipes):
-        chunks = 4
-        return pl.pallas_call(
-            functools.partial(final_kernel, recipes, blocks, len(arrays)),
+    def place(pieces, is_hot):
+        names = sorted({at[piece][0] for piece in pieces})
+        terms = [(names.index(at[piece][0]), at[piece][1]) for piece in pieces]
+        arrays, chunks = [value[name] for name in names], 4
+        out = pl.pallas_call(
+            functools.partial(place_kernel, terms, is_hot, blocks, len(arrays)),
             out_shape=jax.ShapeDtypeStruct((EXP_DEV, ff, width), jnp.bfloat16),
-            in_specs=[SMEM] + [VMEM] * len(arrays),
+            in_specs=[SMEM] + [VMEM] * len(arrays) + [ANY],
             out_specs=HBM,
             scratch_shapes=[
-                pltpu.VMEM((EXP_DEV, chunks, ff // chunks, width), jnp.bfloat16),
-                pltpu.SemaphoreType.DMA((EXP_DEV, chunks)),
+                pltpu.VMEM((chunks, ff // chunks, width), jnp.bfloat16),
+                pltpu.SemaphoreType.DMA((chunks,)),
             ],
+            input_output_aliases={1 + len(arrays): 0} if is_hot else {},
             compiler_params=params(32),
             cost_estimate=cost,
-            name="finish",
-        )(flags, *arrays)
+            name="finish" if is_hot else "sum_f",
+        )(flags, *arrays, value["out"] if is_hot else chain[-1])
+        value["out"] = out
+        if not is_hot:
+            chain.append(out)
+        return out
 
     def plane(x, phase):
         pairs = []
@@ -361,7 +428,8 @@
             (out,) = sums(name, [[("r" + mask, F_GOES), ("p" + mask, F_PASSES)] for mask in masks])
             store("q" + name, plane(out, 1), ["q" + mask for mask in masks])
         elif what == "g":
-            (out,) = sums(name, [gathered(mask) for mask in masks])
+            more = [("my", None)] if masks == "0" else []
+            (out,) = sums(name, [gathered(mask) + more for mask in masks])
             store(name, out, ["g" + mask for mask in masks])
             if masks[0] in "32":
                 store("o" + name, outer(out), ["oh" + mask for mask in masks])
@@ -375,12 +443,11 @@
             (out,) = sums(name, [whole[part] for part in masks])
             store("x" + name, both(out), ["x" + part for part in masks])
         elif what == "z":
-            out, more = sums(name, [gathered("1") + [("mx", None)]], [gathered("0")])
+            out, more = sums(name, [gathered("1") + [("mx", None)]], [gathered("0") + [("my", None)]])
             store("g0", more, ["g0"])
             store("x" + name, both(out), ["xh"])
         elif what == "f":
-            (out,) = sums(name, [[("c0", None), ("mb", None), ("xc", None)]])
-            store("f", out, ["f"])
+            place(["c0", "mb", "xc"], False)
         else:
             names = name.split(",")
             keep(names, product(*groups_of(names)))
@@ -390,10 +457,7 @@
     keep(names, outs)
     for name in ORDER[1:]:
         step(name)
-    lists = [["f"] if "f" in ORDER else ["c0", "mb", "xc"], ["g0", "my", "xh"]]
-    names = sorted({at[piece][0] for pieces in lists for piece in pieces})
-    recipe = [[(names.index(at[piece][0]), at[piece][1]) for piece in pieces] for pieces in lists]
-    return final([value[name] for name in names], recipe)
+    return place(["g0", "xh"], True)
 
 
 def solution(mesh):

time: 114 us -> 114 us (level)
  waiting for transfers between devices: 59.6 us -> 50.3 us
  Pallas kernels: 25.6 us -> 33.1 us
  local copies, waits for them, and re-layouts: 0 us -> 1.41 us
    ppermute x4, waiting for transfers between devices: 25.3 us -> 18.8 us  [outer(): return lax.ppermute(x, 'dp', [(0, 1), (n - 1, n - 2)])]
    pallas_call x3, Pallas kernels: 9.23 us -> 14.7 us  [product(): pl.pallas_call(functools.partial(product_kernel, groups, blocks), out_sha...]
    ppermute x2, waiting for transfers between devices: 19.8 us -> 15.4 us  [both(): return lax.ppermute(x, 'dp', [(0, 1), (1, 0), (2, 3), (3, 2)])]
    ppermute x8, waiting for transfers between devices: 5.3 us -> 8.77 us  [plane(): return lax.ppermute(x, 'expert', pairs)]
    ppermute x4, starting transfers between devices: 10.6 us -> 12.6 us  [middle(): return lax.ppermute(x, 'dp', [(1, 2), (2, 1)])]
    ppermute x8, starting transfers between devices: 11.9 us -> 10 us  [plane(): return lax.ppermute(x, 'expert', pairs)]
    ppermute x4, waiting for transfers between devices: 9.19 us -> 7.42 us  [middle(): return lax.ppermute(x, 'dp', [(1, 2), (2, 1)])]
    pallas_call x1, Pallas kernels: 3.34 us -> 4.79 us  [opening(): pl.pallas_call(functools.partial(opening_kernel, groups, blocks, holders)...]
  transfers between devices with their start and end apart: 18 -> 18, of which waited for: 12 -> 11; matrix products, arithmetic and copies ran while one was open for 0% -> 0% of each run, Pallas kernels for 18% -> 24%
where the time goes in v1:
time: 114 us
  waiting for transfers between devices  50.3 us (44%)
  Pallas kernels  33.1 us (29%)
  starting transfers between devices  27.9 us (24%)
  local copies, waits for them, and re-layouts  1.41 us (1%)
    ppermute x4, waiting for transfers between devices, outer(): return lax.ppermute(x, 'dp', [(0, 1), (n - 1, n - 2)])  18.8 us
    ppermute x2, waiting for transfers between devices, both(): return lax.ppermute(x, 'dp', [(0, 1), (1, 0), (2, 3), (3, 2)])  15.4 us
    pallas_call x3, Pallas kernels, product(): pl.pallas_call(functools.partial(product_kernel, groups, blocks), out_sha...  14.7 us
    ppermute x4, starting transfers between devices, middle(): return lax.ppermute(x, 'dp', [(1, 2), (2, 1)])  12.6 us
    pallas_call x13, Pallas kernels, combine(): pl.pallas_call(functools.partial(combine_kernel, groups, blocks, len(arra...  10.6 us
    ppermute x8, starting transfers between devices, plane(): return lax.ppermute(x, 'expert', pairs)  10 us
    ppermute x8, waiting for transfers between devices, plane(): return lax.ppermute(x, 'expert', pairs)  8.77 us
    ppermute x4, waiting for transfers between devices, middle(): return lax.ppermute(x, 'dp', [(1, 2), (2, 1)])  7.42 us
  transfers between devices with their start and end apart: 18, of which 11 were waited for; matrix products, arithmetic and copies ran while one was open for 0% of the time, Pallas kernels for 24%

profile of v1, /device:TPU:8, one launch (start us, length us, event | category | flops | bytes accessed | tf_op | source)
XLA Modules:
  0.0 113.6 jit_solution(4762140306323891936)
XLA Ops:
  0.7 4.8 %open_c3_r3.1 = (s32[23]{0:T(128)S(1)}, bf16[768,512]{1,0:T(8,128)(2,1)S(1)}, bf16[768,512]{1,0:T(8,128)(2,1)S(1)}) custom-call(s32[1,8]{1,0:T(1,128)} %slots.1, s32[1]{0:T(128)S(6)} %copy.8.counts, s32[8]{0:T(128)} %placement.1, bf16[1024,768]{1,0:T(8,128)(2,1)} %hidden.7, bf16[1024,2048]{1,0:T(8,128)(2,1)} %grad.7), custom_call_target="tpu_custom_call" | custom-call | flops 1 | bytes 1 | tf_op jit(solution)/shard_map/open_c3_r3/pallas_call | solution.py:299
  5.4 0.4 collective-permute-start.1
  5.8 1.3 %collective-permute-start = (bf16[768,512]{1,0:T(8,128)(2,1)S(1)}, bf16[768,512]{1,0:T(8,128)(2,1)S(1)}, u32[]{:S(2)}, u32[]{:S(2)}) collective-permute-start(bf16[768,512]{1,0:T(8,128)(2,1)S(1)} %get-tuple-element.17.refs_0_), channel_id=1, source_target_pairs={{0,8},{24,16},{1,9},{25,17},{2,10},{26,18},{3,11},{27,19},{4,12},{... | collective-permute-start | bytes 2359304 | tf_op jit(solution)/shard_map/ppermute | solution.py:380
  7.1 5.2 %make_c2_c10.1 = (bf16[768,512]{1,0:T(8,128)(2,1)S(1)}, bf16[2,768,512]{2,1,0:T(8,128)(2,1)S(1)}) custom-call(s32[23]{0:T(128)S(1)} %get-tuple-element.16.flags, bf16[1024,768]{1,0:T(8,128)(2,1)} %hidden.7, bf16[1024,2048]{1,0:T(8,128)(2,1)} %grad.7, bf16[768,512]{1,0:T(8,128)(2,1)S(1)} %get-tuple-element.17.refs_0_), custom_call_target="tpu_custom_call" | custom-call | flops 1 | bytes 1 | tf_op jit(solution)/shard_map/make_c2_c10/pallas_call | solution.py:323
  12.3 5.3 %make_r2_r1_r0.1 = (bf16[768,512]{1,0:T(8,128)(2,1)S(1)}, bf16[768,512]{1,0:T(8,128)(2,1)S(1)}, bf16[768,512]{1,0:T(8,128)(2,1)S(1)}) custom-call(s32[23]{0:T(128)S(1)} %get-tuple-element.16.flags, bf16[1024,768]{1,0:T(8,128)(2,1)} %hidden.7, bf16[1024,2048]{1,0:T(8,128)(2,1)} %grad.7, bf16[768,512]{1,0:T(8,128)(2,1)S(1)} %get-tuple-element.18.refs_0_), custom_call_target="tpu_custom_call" | custom-call | flops 1 | bytes 1 | tf_op jit(solution)/shard_map/make_r2_r1_r0/pallas_call | solution.py:323
  17.7 0.1 collective-permute-start.3
  17.7 0.0 collective-permute-done.1.refs_1_
  17.8 0.8 sum_s3.1.refs_2_
  18.6 3.7 %collective-permute-start.7 = (bf16[768,512]{1,0:T(8,128)(2,1)S(1)}, bf16[768,512]{1,0:T(8,128)(2,1)S(1)}, u32[]{:S(2)}, u32[]{:S(2)}) collective-permute-start(bf16[768,512]{1,0:T(8,128)(2,1)S(1)} %sum_s3.1.refs_2_), channel_id=1, source_target_pairs={{0,4},{1,3},{2,6},{3,1},{4,0},{5,7},{6,2},{7,5},{8,12},{9,11},{10,... | collective-permute-start | bytes 2359304 | tf_op jit(solution)/shard_map/ppermute | solution.py:377
  22.3 1.3 %collective-permute-start.6 = (bf16[768,512]{1,0:T(8,128)(2,1)S(1)}, bf16[768,512]{1,0:T(8,128)(2,1)S(1)}, u32[]{:S(2)}, u32[]{:S(2)}) collective-permute-start(bf16[768,512]{1,0:T(8,128)(2,1)S(1)} %get-tuple-element.18.refs_0_), channel_id=1, source_target_pairs={{0,8},{24,16},{1,9},{25,17},{2,10},{26,18},{3,11},{27,19},{4,12},{... | collective-permute-start | bytes 2359304 | tf_op jit(solution)/shard_map/ppermute | solution.py:380
  23.6 4.6 %collective-permute-done.refs_1_ = bf16[768,512]{1,0:T(8,128)(2,1)S(1)} collective-permute-done((bf16[768,512]{1,0:T(8,128)(2,1)S(1)}, bf16[768,512]{1,0:T(8,128)(2,1)S(1)}, u32[]{:S(2)}, u32[]{:S(2)}) %collective-permute-start) | collective-permute-done | bytes 786464 | tf_op jit(solution)/shard_map/ppermute | solution.py:380
  28.1 0.7 sum_ma.1.refs_0_
  28.9 3.5 %collective-permute-start.5 = (bf16[768,512]{1,0:T(8,128)(2,1)S(1)}, bf16[768,512]{1,0:T(8,128)(2,1)S(1)}, u32[]{:S(2)}, u32[]{:S(2)}) collective-permute-start(bf16[768,512]{1,0:T(8,128)(2,1)S(1)} %sum_ma.1.refs_0_), channel_id=1, source_target_pairs={{8,16},{16,8},{9,17},{17,9},{10,18},{18,10},{11,19},{19,11},{12,20... | collective-permute-start | bytes 2359304 | tf_op jit(solution)/shard_map/ppermute | solution.py:383
  32.4 4.2 %make_h3_h2_h10.1 = (bf16[768,512]{1,0:T(8,128)(2,1)S(1)}, bf16[768,512]{1,0:T(8,128)(2,1)S(1)}, bf16[2,768,512]{2,1,0:T(8,128)(2,1)S(1)}) custom-call(s32[23]{0:T(128)S(1)} %get-tuple-element.16.flags, bf16[1024,768]{1,0:T(8,128)(2,1)} %hidden.7, bf16[1024,2048]{1,0:T(8,128)(2,1)} %grad.7, bf16[768,512]{1,0:T(8,128)(2,1)S(1)} %sum_ma.1.refs_0_), custom_call_target="tpu_custom_call" | custom-call | flops 1 | bytes 1 | tf_op jit(solution)/shard_map/make_h3_h2_h10/pallas_call | solution.py:323
  36.6 1.1 collective-permute-done.3.refs_1_
  37.7 0.8 sum_s2.1.refs_3_
  38.6 1.9 %collective-permute-start.4 = (bf16[768,512]{1,0:T(8,128)(2,1)S(1)}, bf16[768,512]{1,0:T(8,128)(2,1)S(1)}, u32[]{:S(2)}, u32[]{:S(2)}) collective-permute-start(bf16[768,512]{1,0:T(8,128)(2,1)S(1)} %sum_s2.1.refs_3_), channel_id=1, source_target_pairs={{0,4},{1,3},{2,6},{3,1},{4,0},{5,7},{6,2},{7,5},{8,12},{9,11},{10,... | collective-permute-start | bytes 2359304 | tf_op jit(solution)/shard_map/ppermute | solution.py:377
  40.4 0.2 collective-permute-start.9
  40.6 0.9 sum_g3.1.refs_2_.refs_0_
  41.5 1.3 %collective-permute-start.8 = (bf16[768,512]{1,0:T(8,128)(2,1)S(1)}, bf16[768,512]{1,0:T(8,128)(2,1)S(1)}, u32[]{:S(2)}, u32[]{:S(2)}) collective-permute-start(bf16[768,512]{1,0:T(8,128)(2,1)S(1)} %sum_g3.1.refs_2_.refs_0_), channel_id=1, source_target_pairs={{0,8},{24,16},{1,9},{25,17},{2,10},{26,18},{3,11},{27,19},{4,12},{... | collective-permute-start | bytes 2359304 | tf_op jit(solution)/shard_map/ppermute | solution.py:380
  42.8 2.2 %collective-permute-done.6.refs_1_ = bf16[768,512]{1,0:T(8,128)(2,1)S(1)} collective-permute-done((bf16[768,512]{1,0:T(8,128)(2,1)S(1)}, bf16[768,512]{1,0:T(8,128)(2,1)S(1)}, u32[]{:S(2)}, u32[]{:S(2)}) %collective-permute-start.6) | collective-permute-done | bytes 786464 | tf_op jit(solution)/shard_map/ppermute | solution.py:380
  45.0 0.7 sum_mb.1.refs_2_
  45.7 4.0 %collective-permute-done.5.refs_1_ = bf16[768,512]{1,0:T(8,128)(2,1)S(1)} collective-permute-done((bf16[768,512]{1,0:T(8,128)(2,1)S(1)}, bf16[768,512]{1,0:T(8,128)(2,1)S(1)}, u32[]{:S(2)}, u32[]{:S(2)}) %collective-permute-start.5) | collective-permute-done | bytes 786464 | tf_op jit(solution)/shard_map/ppermute | solution.py:383
  49.8 2.2 %collective-permute-start.12 = (bf16[768,512]{1,0:T(8,128)(2,1)S(1)}, bf16[768,512]{1,0:T(8,128)(2,1)S(1)}, u32[]{:S(2)}, u32[]{:S(2)}) collective-permute-start(bf16[768,512]{1,0:T(8,128)(2,1)S(1)} %sum_mb.1.refs_2_), channel_id=1, source_target_pairs={{8,16},{16,8},{9,17},{17,9},{10,18},{18,10},{11,19},{19,11},{12,20... | collective-permute-start | bytes 2359304 | tf_op jit(solution)/shard_map/ppermute | solution.py:383
  52.0 0.7 sum_xc.1.refs_3_
  52.7 6.3 %collective-permute-done.4.refs_2_ = bf16[768,512]{1,0:T(8,128)(2,1)S(1)} collective-permute-done((bf16[768,512]{1,0:T(8,128)(2,1)S(1)}, bf16[768,512]{1,0:T(8,128)(2,1)S(1)}, u32[]{:S(2)}, u32[]{:S(2)}) %collective-permute-start.4) | collective-permute-done | bytes 786464 | tf_op jit(solution)/shard_map/ppermute | solution.py:377
  59.0 0.9 sum_g2.1.refs_2_.refs_0_
  59.9 1.3 %collective-permute-start.11 = (bf16[768,512]{1,0:T(8,128)(2,1)S(1)}, bf16[768,512]{1,0:T(8,128)(2,1)S(1)}, u32[]{:S(2)}, u32[]{:S(2)}) collective-permute-start(bf16[768,512]{1,0:T(8,128)(2,1)S(1)} %sum_g2.1.refs_2_.refs_0_), channel_id=1, source_target_pairs={{0,8},{24,16},{1,9},{25,17},{2,10},{26,18},{3,11},{27,19},{4,12},{... | collective-permute-start | bytes 2359304 | tf_op jit(solution)/shard_map/ppermute | solution.py:380
  61.2 0.8 sum_s1.1.refs_2_
  62.0 1.9 %collective-permute-start.15 = (bf16[768,512]{1,0:T(8,128)(2,1)S(1)}, bf16[768,512]{1,0:T(8,128)(2,1)S(1)}, u32[]{:S(2)}, u32[]{:S(2)}) collective-permute-start(bf16[768,512]{1,0:T(8,128)(2,1)S(1)} %sum_s1.1.refs_2_), channel_id=1, source_target_pairs={{0,4},{1,3},{2,6},{3,1},{4,0},{5,7},{6,2},{7,5},{8,12},{9,11},{10,... | collective-permute-start | bytes 2359304 | tf_op jit(solution)/shard_map/ppermute | solution.py:377
  64.0 0.7 sum_mx.1.refs_2_
  64.7 3.5 %collective-permute-start.16 = (bf16[768,512]{1,0:T(8,128)(2,1)S(1)}, bf16[768,512]{1,0:T(8,128)(2,1)S(1)}, u32[]{:S(2)}, u32[]{:S(2)}) collective-permute-start(bf16[768,512]{1,0:T(8,128)(2,1)S(1)} %sum_mx.1.refs_2_), channel_id=1, source_target_pairs={{8,16},{16,8},{9,17},{17,9},{10,18},{18,10},{11,19},{19,11},{12,20... | collective-permute-start | bytes 2359304 | tf_op jit(solution)/shard_map/ppermute | solution.py:383
  68.2 1.3 %collective-permute-done.2.refs_1_ = bf16[768,512]{1,0:T(8,128)(2,1)S(1)} collective-permute-done((bf16[768,512]{1,0:T(8,128)(2,1)S(1)}, bf16[768,512]{1,0:T(8,128)(2,1)S(1)}, u32[]{:S(2)}, u32[]{:S(2)}) %collective-permute-start.2) | collective-permute-done | bytes 786464 | tf_op jit(solution)/shard_map/ppermute | solution.py:377
  69.5 0.8 sum_s0.1.refs_2_
  70.3 12.0 %collective-permute-done.11.refs_1_ = bf16[768,512]{1,0:T(8,128)(2,1)S(1)} collective-permute-done((bf16[768,512]{1,0:T(8,128)(2,1)S(1)}, bf16[768,512]{1,0:T(8,128)(2,1)S(1)}, u32[]{:S(2)}, u32[]{:S(2)}) %collective-permute-start.11) | collective-permute-done | bytes 786464 | tf_op jit(solution)/shard_map/ppermute | solution.py:380
  82.3 1.9 %collective-permute-start.10 = (bf16[768,512]{1,0:T(8,128)(2,1)S(1)}, bf16[768,512]{1,0:T(8,128)(2,1)S(1)}, u32[]{:S(2)}, u32[]{:S(2)}) collective-permute-start(bf16[768,512]{1,0:T(8,128)(2,1)S(1)} %sum_s0.1.refs_2_), channel_id=1, source_target_pairs={{0,4},{1,3},{2,6},{3,1},{4,0},{5,7},{6,2},{7,5},{8,12},{9,11},{10,... | collective-permute-start | bytes 2359304 | tf_op jit(solution)/shard_map/ppermute | solution.py:377
  84.2 0.7 sum_my.1.refs_4_
  84.9 3.5 %collective-permute-start.13 = (bf16[768,512]{1,0:T(8,128)(2,1)S(1)}, bf16[768,512]{1,0:T(8,128)(2,1)S(1)}, u32[]{:S(2)}, u32[]{:S(2)}) collective-permute-start(bf16[768,512]{1,0:T(8,128)(2,1)S(1)} %sum_my.1.refs_4_), channel_id=1, source_target_pairs={{8,16},{16,8},{9,17},{17,9},{10,18},{18,10},{11,19},{19,11},{12,20... | collective-permute-start | bytes 2359304 | tf_op jit(solution)/shard_map/ppermute | solution.py:383
  88.4 0.6 collective-permute-done.16.refs_3_
  89.0 1.0 sum_xh.1.refs_3_
  90.0 0.1 collective-permute-start.17
  90.0 9.1 %collective-permute-done.14.refs_2_ = bf16[768,512]{1,0:T(8,128)(2,1)S(1)} collective-permute-done((bf16[768,512]{1,0:T(8,128)(2,1)S(1)}, bf16[768,512]{1,0:T(8,128)(2,1)S(1)}, u32[]{:S(2)}, u32[]{:S(2)}) %collective-permute-start.14) | collective-permute-done | bytes 786464 | tf_op jit(solution)/shard_map/ppermute | solution.py:386
  99.1 1.5 %sum_f.1.refs_4_.refs_2_ = bf16[2,768,512]{2,1,0:T(8,128)(2,1)} custom-call(s32[23]{0:T(128)S(1)} %get-tuple-element.16.flags, bf16[2,768,512]{2,1,0:T(8,128)(2,1)S(1)} %get-tuple-element.25.refs_0_, bf16[768,512]{1,0:T(8,128)(2,1)S(1)} %collective-permute-done.12.refs_3_.refs_1_, bf16[768,512]{1,0:T(8,128)(2,1)S(1)} %collective-permute-done.14.refs_2_, ...), custom_call_target="tpu_custom_call" | custom-call | flops 1 | bytes 1 | tf_op jit(solution)/shard_map/sum_f/pallas_call | solution.py:353
  100.7 2.8 %collective-permute-done.13.refs_3_ = bf16[768,512]{1,0:T(8,128)(2,1)S(1)} collective-permute-done((bf16[768,512]{1,0:T(8,128)(2,1)S(1)}, bf16[768,512]{1,0:T(8,128)(2,1)S(1)}, u32[]{:S(2)}, u32[]{:S(2)}) %collective-permute-start.13) | collective-permute-done | bytes 786464 | tf_op jit(solution)/shard_map/ppermute | solution.py:383
  103.4 1.4 %copy-done = bf16[2,768,512]{2,1,0:T(8,128)(2,1)S(1)} copy-done((bf16[2,768,512]{2,1,0:T(8,128)(2,1)S(1)}, bf16[2,768,512]{2,1,0:T(8,128)(2,1)}, u32[]{:S(2)}) %copy-start) | copy-done | bytes 1572888
  104.9 1.0 sum_g0.1.refs_0_
  105.8 6.3 %collective-permute-done.17.refs_1_ = bf16[768,512]{1,0:T(8,128)(2,1)S(1)} collective-permute-done((bf16[768,512]{1,0:T(8,128)(2,1)S(1)}, bf16[768,512]{1,0:T(8,128)(2,1)S(1)}, u32[]{:S(2)}, u32[]{:S(2)}) %collective-permute-start.17) | collective-permute-done | bytes 786464 | tf_op jit(solution)/shard_map/ppermute | solution.py:386
  112.1 1.5 %finish.1 = bf16[2,768,512]{2,1,0:T(8,128)(2,1)} custom-call(s32[23]{0:T(128)S(1)} %get-tuple-element.16.flags, bf16[768,512]{1,0:T(8,128)(2,1)S(1)} %sum_g0.1.refs_0_, bf16[768,512]{1,0:T(8,128)(2,1)S(1)} %collective-permute-done.17.refs_1_, bf16[2,768,512]{2,1,0:T(8,128)(2,1)} %sum_f.1.refs_4_.refs_2_), custom_call_target="tpu_custom_call", output_to_operand_aliasing={{}: (3, {})} | custom-call | flops 1 | bytes 1 | tf_op jit(solution)/shard_map/finish/pallas_call | solution.py:353
  (9 shorter events, 0.0 us)
Async XLA Ops:
  5.4 12.3 %collective-permute-start.1 = (bf16[768,512]{1,0:T(8,128)(2,1)S(1)}, bf16[768,512]{1,0:T(8,128)(2,1)S(1)}, u32[]{:S(2)}, u32[]{:S(2)}) collective-permute-start(bf16[768,512]{1,0:T(8,128)(2,1)S(1)} %get-tuple-element.19.refs_0_), channel_id=1, source_target_pairs={{0,2},{1,5},{2,0},{3,7},{4,6},{5,1},{6,4},{7,3},{8,10},{9,13},{10,... | collective-permute-start | bytes 2359304 | tf_op jit(solution)/shard_map/ppermute | solution.py:377
  5.8 22.3 %collective-permute-start = (bf16[768,512]{1,0:T(8,128)(2,1)S(1)}, bf16[768,512]{1,0:T(8,128)(2,1)S(1)}, u32[]{:S(2)}, u32[]{:S(2)}) collective-permute-start(bf16[768,512]{1,0:T(8,128)(2,1)S(1)} %get-tuple-element.17.refs_0_), channel_id=1, source_target_pairs={{0,8},{24,16},{1,9},{25,17},{2,10},{26,18},{3,11},{27,19},{4,12},{... | collective-permute-start | bytes 2359304 | tf_op jit(solution)/shard_map/ppermute | solution.py:380
  17.7 20.1 %collective-permute-start.3 = (bf16[768,512]{1,0:T(8,128)(2,1)S(1)}, bf16[768,512]{1,0:T(8,128)(2,1)S(1)}, u32[]{:S(2)}, u32[]{:S(2)}) collective-permute-start(bf16[768,512]{1,0:T(8,128)(2,1)S(1)} %get-tuple-element.20.refs_2_.refs_0_), channel_id=1, source_target_pairs={{0,2},{1,5},{2,0},{3,7},{4,6},{5,1},{6,4},{7,3},{8,10},{9,13},{10,... | collective-permute-start | bytes 2359304 | tf_op jit(solution)/shard_map/ppermute | solution.py:377
  18.6 22.0 %collective-permute-start.7 = (bf16[768,512]{1,0:T(8,128)(2,1)S(1)}, bf16[768,512]{1,0:T(8,128)(2,1)S(1)}, u32[]{:S(2)}, u32[]{:S(2)}) collective-permute-start(bf16[768,512]{1,0:T(8,128)(2,1)S(1)} %sum_s3.1.refs_2_), channel_id=1, source_target_pairs={{0,4},{1,3},{2,6},{3,1},{4,0},{5,7},{6,2},{7,5},{8,12},{9,11},{10,... | collective-permute-start | bytes 2359304 | tf_op jit(solution)/shard_map/ppermute | solution.py:377
  22.3 22.7 %collective-permute-start.6 = (bf16[768,512]{1,0:T(8,128)(2,1)S(1)}, bf16[768,512]{1,0:T(8,128)(2,1)S(1)}, u32[]{:S(2)}, u32[]{:S(2)}) collective-permute-start(bf16[768,512]{1,0:T(8,128)(2,1)S(1)} %get-tuple-element.18.refs_0_), channel_id=1, source_target_pairs={{0,8},{24,16},{1,9},{25,17},{2,10},{26,18},{3,11},{27,19},{4,12},{... | collective-permute-start | bytes 2359304 | tf_op jit(solution)/shard_map/ppermute | solution.py:380
  28.9 20.9 %collective-permute-start.5 = (bf16[768,512]{1,0:T(8,128)(2,1)S(1)}, bf16[768,512]{1,0:T(8,128)(2,1)S(1)}, u32[]{:S(2)}, u32[]{:S(2)}) collective-permute-start(bf16[768,512]{1,0:T(8,128)(2,1)S(1)} %sum_ma.1.refs_0_), channel_id=1, source_target_pairs={{8,16},{16,8},{9,17},{17,9},{10,18},{18,10},{11,19},{19,11},{12,20... | collective-permute-start | bytes 2359304 | tf_op jit(solution)/shard_map/ppermute | solution.py:383
  38.6 20.5 %collective-permute-start.4 = (bf16[768,512]{1,0:T(8,128)(2,1)S(1)}, bf16[768,512]{1,0:T(8,128)(2,1)S(1)}, u32[]{:S(2)}, u32[]{:S(2)}) collective-permute-start(bf16[768,512]{1,0:T(8,128)(2,1)S(1)} %sum_s2.1.refs_3_), channel_id=1, source_target_pairs={{0,4},{1,3},{2,6},{3,1},{4,0},{5,7},{6,2},{7,5},{8,12},{9,11},{10,... | collective-permute-start | bytes 2359304 | tf_op jit(solution)/shard_map/ppermute | solution.py:377
  40.4 20.8 %collective-permute-start.9 = (bf16[768,512]{1,0:T(8,128)(2,1)S(1)}, bf16[768,512]{1,0:T(8,128)(2,1)S(1)}, u32[]{:S(2)}, u32[]{:S(2)}) collective-permute-start(bf16[768,512]{1,0:T(8,128)(2,1)S(1)} %get-tuple-element.26.refs_0_), channel_id=1, source_target_pairs={{0,2},{1,5},{2,0},{3,7},{4,6},{5,1},{6,4},{7,3},{8,10},{9,13},{10,... | collective-permute-start | bytes 2359304 | tf_op jit(solution)/shard_map/ppermute | solution.py:377
  41.5 22.5 %collective-permute-start.8 = (bf16[768,512]{1,0:T(8,128)(2,1)S(1)}, bf16[768,512]{1,0:T(8,128)(2,1)S(1)}, u32[]{:S(2)}, u32[]{:S(2)}) collective-permute-start(bf16[768,512]{1,0:T(8,128)(2,1)S(1)} %sum_g3.1.refs_2_.refs_0_), channel_id=1, source_target_pairs={{0,8},{24,16},{1,9},{25,17},{2,10},{26,18},{3,11},{27,19},{4,12},{... | collective-permute-start | bytes 2359304 | tf_op jit(solution)/shard_map/ppermute | solution.py:380
  45.0 24.5 %collective-permute-start.2 = (bf16[768,512]{1,0:T(8,128)(2,1)S(1)}, bf16[768,512]{1,0:T(8,128)(2,1)S(1)}, u32[]{:S(2)}, u32[]{:S(2)}) collective-permute-start(bf16[768,512]{1,0:T(8,128)(2,1)S(1)} %get-tuple-element.22.refs_0_), channel_id=1, source_target_pairs={{0,2},{1,5},{2,0},{3,7},{4,6},{5,1},{6,4},{7,3},{8,10},{9,13},{10,... | collective-permute-start | bytes 2359304 | tf_op jit(solution)/shard_map/ppermute | solution.py:377
  49.8 34.4 %collective-permute-start.12 = (bf16[768,512]{1,0:T(8,128)(2,1)S(1)}, bf16[768,512]{1,0:T(8,128)(2,1)S(1)}, u32[]{:S(2)}, u32[]{:S(2)}) collective-permute-start(bf16[768,512]{1,0:T(8,128)(2,1)S(1)} %sum_mb.1.refs_2_), channel_id=1, source_target_pairs={{8,16},{16,8},{9,17},{17,9},{10,18},{18,10},{11,19},{19,11},{12,20... | collective-permute-start | bytes 2359304 | tf_op jit(solution)/shard_map/ppermute | solution.py:383
  59.9 22.4 %collective-permute-start.11 = (bf16[768,512]{1,0:T(8,128)(2,1)S(1)}, bf16[768,512]{1,0:T(8,128)(2,1)S(1)}, u32[]{:S(2)}, u32[]{:S(2)}) collective-permute-start(bf16[768,512]{1,0:T(8,128)(2,1)S(1)} %sum_g2.1.refs_2_.refs_0_), channel_id=1, source_target_pairs={{0,8},{24,16},{1,9},{25,17},{2,10},{26,18},{3,11},{27,19},{4,12},{... | collective-permute-start | bytes 2359304 | tf_op jit(solution)/shard_map/ppermute | solution.py:380
  62.0 26.3 %collective-permute-start.15 = (bf16[768,512]{1,0:T(8,128)(2,1)S(1)}, bf16[768,512]{1,0:T(8,128)(2,1)S(1)}, u32[]{:S(2)}, u32[]{:S(2)}) collective-permute-start(bf16[768,512]{1,0:T(8,128)(2,1)S(1)} %sum_s1.1.refs_2_), channel_id=1, source_target_pairs={{0,4},{1,3},{2,6},{3,1},{4,0},{5,7},{6,2},{7,5},{8,12},{9,11},{10,... | collective-permute-start | bytes 2359304 | tf_op jit(solution)/shard_map/ppermute | solution.py:377
  64.7 24.3 %collective-permute-start.16 = (bf16[768,512]{1,0:T(8,128)(2,1)S(1)}, bf16[768,512]{1,0:T(8,128)(2,1)S(1)}, u32[]{:S(2)}, u32[]{:S(2)}) collective-permute-start(bf16[768,512]{1,0:T(8,128)(2,1)S(1)} %sum_mx.1.refs_2_), channel_id=1, source_target_pairs={{8,16},{16,8},{9,17},{17,9},{10,18},{18,10},{11,19},{19,11},{12,20... | collective-permute-start | bytes 2359304 | tf_op jit(solution)/shard_map/ppermute | solution.py:383
  69.5 29.6 %collective-permute-start.14 = (bf16[768,512]{1,0:T(8,128)(2,1)S(1)}, bf16[768,512]{1,0:T(8,128)(2,1)S(1)}, u32[]{:S(2)}, u32[]{:S(2)}) collective-permute-start(bf16[768,512]{1,0:T(8,128)(2,1)S(1)} %sum_xc.1.refs_3_), channel_id=1, source_target_pairs={{0,8},{8,0},{16,24},{24,16},{1,9},{9,1},{17,25},{25,17},{2,10},{10... | collective-permute-start | bytes 2359304 | tf_op jit(solution)/shard_map/ppermute | solution.py:386
  82.3 21.2 %collective-permute-start.10 = (bf16[768,512]{1,0:T(8,128)(2,1)S(1)}, bf16[768,512]{1,0:T(8,128)(2,1)S(1)}, u32[]{:S(2)}, u32[]{:S(2)}) collective-permute-start(bf16[768,512]{1,0:T(8,128)(2,1)S(1)} %sum_s0.1.refs_2_), channel_id=1, source_target_pairs={{0,4},{1,3},{2,6},{3,1},{4,0},{5,7},{6,2},{7,5},{8,12},{9,11},{10,... | collective-permute-start | bytes 2359304 | tf_op jit(solution)/shard_map/ppermute | solution.py:377
  84.9 18.5 %collective-permute-start.13 = (bf16[768,512]{1,0:T(8,128)(2,1)S(1)}, bf16[768,512]{1,0:T(8,128)(2,1)S(1)}, u32[]{:S(2)}, u32[]{:S(2)}) collective-permute-start(bf16[768,512]{1,0:T(8,128)(2,1)S(1)} %sum_my.1.refs_4_), channel_id=1, source_target_pairs={{8,16},{16,8},{9,17},{17,9},{10,18},{18,10},{11,19},{19,11},{12,20... | collective-permute-start | bytes 2359304 | tf_op jit(solution)/shard_map/ppermute | solution.py:383
  90.0 22.2 %collective-permute-start.17 = (bf16[768,512]{1,0:T(8,128)(2,1)S(1)}, bf16[768,512]{1,0:T(8,128)(2,1)S(1)}, u32[]{:S(2)}, u32[]{:S(2)}) collective-permute-start(bf16[768,512]{1,0:T(8,128)(2,1)S(1)} %sum_xh.1.refs_3_), channel_id=1, source_target_pairs={{0,8},{8,0},{16,24},{24,16},{1,9},{9,1},{17,25},{25,17},{2,10},{10... | collective-permute-start | bytes 2359304 | tf_op jit(solution)/shard_map/ppermute | solution.py:386
  103.4 1.4 %copy-start = (bf16[2,768,512]{2,1,0:T(8,128)(2,1)S(1)}, bf16[2,768,512]{2,1,0:T(8,128)(2,1)}, u32[]{:S(2)}) copy-start(bf16[2,768,512]{2,1,0:T(8,128)(2,1)} %sum_f.1.refs_4_.refs_2_) | copy-start | bytes 4718596

commit v2 on v1

--- a/solution.py
+++ b/solution.py
@@ -8,7 +8,7 @@
 from jax.sharding import PartitionSpec as P
 
 EXP_DEV = 2
-ORDER = ("c3,r3", "c2,c10", "r2,r1,r0", "s3", "ma", "h3,h2,h10", "s2", "g3", "mb", "xc", "g2", "s1", "mx", "s0", "my@mb", "xh", "f", "g0")
+ORDER = ("c3,r3", "c2,c103", "r2,r1,r0", "s3", "ma", "h3,h2,h10", "s2", "g3", "mb", "xc", "g2", "s1", "mx", "s0", "my@mb", "xh", "f", "g0")
 COLD, HOT, REPLICA = 0, 1, 2
 SMEM = pl.BlockSpec(memory_space=pltpu.SMEM)
 VMEM = pl.BlockSpec(memory_space=pltpu.VMEM)
@@ -178,13 +178,18 @@
         copy.wait()
     for (kind, _), out in zip(found, outs):
         count = flags[blocks + F_BLOCKS + kind]
+        if kind == COLD:
+            here, n = lax.axis_index("dp"), lax.axis_size("dp")
+            count = jnp.where((here == 0) | (here == n - 1), count, 0)
 
         @pl.when(count == 0)
         def _(out=out):
             out[...] = jnp.zeros(out.shape, out.dtype)
 
-        @pl.loop(0, lax.div(count + 1, 2))
-        def _(i, kind=kind, count=count):
+        pairs = lax.div(count + 1, 2)
+
+        @pl.loop(0, pairs)
+        def _(i, kind=kind, count=count, out=out, end=pairs - 1):
             for half in range(2):
                 mine = slice(half * rows, (half + 1) * rows)
 
@@ -206,17 +211,21 @@
             def product():
                 return jnp.dot(turned[...], pair[...], preferred_element_type=jnp.float32)
 
-            @pl.when(i == 0)
+            @pl.when((i == 0) & (i < end))
             def _():
                 total[...] = product()
 
-            @pl.when(i > 0)
+            @pl.when((i > 0) & (i < end))
             def _():
                 total[...] += product()
 
-        @pl.when(count > 0)
-        def _(out=out):
-            out[...] = total[...].astype(out.dtype)
+            @pl.when((i == 0) & (i == end))
+            def _():
+                out[...] = product().astype(out.dtype)
+
+            @pl.when((i > 0) & (i == end))
+            def _():
+                out[...] = (total[...] + product()).astype(out.dtype)
 
 
 def product_kernel(groups, blocks, flags, hidden, grad, *refs):

time: 114 us -> 115 us (level)
  starting transfers between devices: 27.9 us -> 36.9 us
  Pallas kernels: 33.1 us -> 26.7 us
  waiting for transfers between devices: 50.3 us -> 48 us
    ppermute x4, waiting for transfers between devices: 7.42 us -> 15.9 us  [middle(): return lax.ppermute(x, 'dp', [(1, 2), (2, 1)])]
    ppermute x8, waiting for transfers between devices: 8.77 us -> 2.03 us  [plane(): return lax.ppermute(x, 'expert', pairs)]
    ppermute x4, starting transfers between devices: 12.6 us -> 17.4 us  [middle(): return lax.ppermute(x, 'dp', [(1, 2), (2, 1)])]
    pallas_call x3, Pallas kernels: 14.7 us -> 10 us  [product(): pl.pallas_call(functools.partial(product_kernel, groups, blocks), out_sha...]
    ppermute x2, waiting for transfers between devices: 15.4 us -> 11.2 us  [both(): return lax.ppermute(x, 'dp', [(0, 1), (1, 0), (2, 3), (3, 2)])]
    ppermute x2, starting transfers between devices: 0.07 us -> 3.84 us  [both(): return lax.ppermute(x, 'dp', [(0, 1), (1, 0), (2, 3), (3, 2)])]
    pallas_call x1, Pallas kernels: 4.79 us -> 3.04 us  [opening(): pl.pallas_call(functools.partial(opening_kernel, groups, blocks, holders)...]
  transfers between devices with their start and end apart: 18 -> 18, of which waited for: 11 -> 10; matrix products, arithmetic and copies ran while one was open for 0% -> 0% of each run, Pallas kernels for 24% -> 19%
where the time goes in v2:
time: 115 us; the launch traced here: 114 us
  waiting for transfers between devices  48 us (42%)
  starting transfers between devices  36.9 us (32%)
  Pallas kernels  26.7 us (23%)
  local copies, waits for them, and re-layouts  1.41 us (1%)
    ppermute x4, waiting for transfers between devices, outer(): return lax.ppermute(x, 'dp', [(0, 1), (n - 1, n - 2)])  18.8 us
    ppermute x4, starting transfers between devices, middle(): return lax.ppermute(x, 'dp', [(1, 2), (2, 1)])  17.4 us
    ppermute x4, waiting for transfers between devices, middle(): return lax.ppermute(x, 'dp', [(1, 2), (2, 1)])  15.9 us
    ppermute x2, waiting for transfers between devices, both(): return lax.ppermute(x, 'dp', [(0, 1), (1, 0), (2, 3), (3, 2)])  11.2 us
    pallas_call x13, Pallas kernels, combine(): pl.pallas_call(functools.partial(combine_kernel, groups, blocks, len(arra...  10.6 us
    ppermute x8, starting transfers between devices, plane(): return lax.ppermute(x, 'expert', pairs)  10.4 us
    pallas_call x3, Pallas kernels, product(): pl.pallas_call(functools.partial(product_kernel, groups, blocks), out_sha...  10 us
    ppermute x4, starting transfers between devices, outer(): return lax.ppermute(x, 'dp', [(0, 1), (n - 1, n - 2)])  5.14 us
  transfers between devices with their start and end apart: 18, of which 10 were waited for; matrix products, arithmetic and copies ran while one was open for 0% of the time, Pallas kernels for 19%

profile of v2, /device:TPU:8, one launch (start us, length us, event | category | flops | bytes accessed | tf_op | source)
XLA Modules:
  0.0 113.8 jit_solution(508067002407864695)
XLA Ops:
  0.7 3.0 %open_c3_r3.1 = (s32[23]{0:T(128)S(1)}, bf16[768,512]{1,0:T(8,128)(2,1)S(1)}, bf16[768,512]{1,0:T(8,128)(2,1)S(1)}) custom-call(s32[1,8]{1,0:T(1,128)} %slots.1, s32[1]{0:T(128)S(6)} %copy.8.counts, s32[8]{0:T(128)} %placement.1, bf16[1024,768]{1,0:T(8,128)(2,1)} %hidden.7, bf16[1024,2048]{1,0:T(8,128)(2,1)} %grad.7), custom_call_target="tpu_custom_call" | custom-call | flops 1 | bytes 1 | tf_op jit(solution)/shard_map/open_c3_r3/pallas_call | solution.py:308
  3.7 1.6 %collective-permute-start.1 = (bf16[768,512]{1,0:T(8,128)(2,1)S(1)}, bf16[768,512]{1,0:T(8,128)(2,1)S(1)}, u32[]{:S(2)}, u32[]{:S(2)}) collective-permute-start(bf16[768,512]{1,0:T(8,128)(2,1)S(1)} %get-tuple-element.19.refs_0_), channel_id=1, source_target_pairs={{0,2},{1,5},{2,0},{3,7},{4,6},{5,1},{6,4},{7,3},{8,10},{9,13},{10,... | collective-permute-start | bytes 2359304 | tf_op jit(solution)/shard_map/ppermute | solution.py:386
  5.3 1.3 %collective-permute-start = (bf16[768,512]{1,0:T(8,128)(2,1)S(1)}, bf16[768,512]{1,0:T(8,128)(2,1)S(1)}, u32[]{:S(2)}, u32[]{:S(2)}) collective-permute-start(bf16[768,512]{1,0:T(8,128)(2,1)S(1)} %get-tuple-element.17.refs_0_), channel_id=1, source_target_pairs={{0,8},{24,16},{1,9},{25,17},{2,10},{26,18},{3,11},{27,19},{4,12},{... | collective-permute-start | bytes 2359304 | tf_op jit(solution)/shard_map/ppermute | solution.py:389
  6.5 4.3 %make_c2_c103.1 = (bf16[768,512]{1,0:T(8,128)(2,1)S(1)}, bf16[3,768,512]{2,1,0:T(8,128)(2,1)S(1)}) custom-call(s32[23]{0:T(128)S(1)} %get-tuple-element.16.flags, bf16[1024,768]{1,0:T(8,128)(2,1)} %hidden.7, bf16[1024,2048]{1,0:T(8,128)(2,1)} %grad.7, bf16[768,512]{1,0:T(8,128)(2,1)S(1)} %get-tuple-element.17.refs_0_), custom_call_target="tpu_custom_call" | custom-call | flops 1 | bytes 1 | tf_op jit(solution)/shard_map/make_c2_c103/pallas_call | solution.py:332
  10.9 3.7 %make_r2_r1_r0.1 = (bf16[768,512]{1,0:T(8,128)(2,1)S(1)}, bf16[768,512]{1,0:T(8,128)(2,1)S(1)}, bf16[768,512]{1,0:T(8,128)(2,1)S(1)}) custom-call(s32[23]{0:T(128)S(1)} %get-tuple-element.16.flags, bf16[1024,768]{1,0:T(8,128)(2,1)} %hidden.7, bf16[1024,2048]{1,0:T(8,128)(2,1)} %grad.7, bf16[768,512]{1,0:T(8,128)(2,1)S(1)} %get-tuple-element.18.refs_0_), custom_call_target="tpu_custom_call" | custom-call | flops 1 | bytes 1 | tf_op jit(solution)/shard_map/make_r2_r1_r0/pallas_call | solution.py:332
  14.6 0.4 collective-permute-start.3
  15.0 0.7 collective-permute-done.1.refs_1_
  15.8 0.8 sum_s3.1.refs_2_
  16.6 2.5 %collective-permute-start.7 = (bf16[768,512]{1,0:T(8,128)(2,1)S(1)}, bf16[768,512]{1,0:T(8,128)(2,1)S(1)}, u32[]{:S(2)}, u32[]{:S(2)}) collective-permute-start(bf16[768,512]{1,0:T(8,128)(2,1)S(1)} %sum_s3.1.refs_2_), channel_id=1, source_target_pairs={{0,4},{1,3},{2,6},{3,1},{4,0},{5,7},{6,2},{7,5},{8,12},{9,11},{10,... | collective-permute-start | bytes 2359304 | tf_op jit(solution)/shard_map/ppermute | solution.py:386
  19.1 1.3 %collective-permute-start.6 = (bf16[768,512]{1,0:T(8,128)(2,1)S(1)}, bf16[768,512]{1,0:T(8,128)(2,1)S(1)}, u32[]{:S(2)}, u32[]{:S(2)}) collective-permute-start(bf16[768,512]{1,0:T(8,128)(2,1)S(1)} %get-tuple-element.18.refs_0_), channel_id=1, source_target_pairs={{0,8},{24,16},{1,9},{25,17},{2,10},{26,18},{3,11},{27,19},{4,12},{... | collective-permute-start | bytes 2359304 | tf_op jit(solution)/shard_map/ppermute | solution.py:389
  20.4 7.1 %collective-permute-done.refs_1_ = bf16[768,512]{1,0:T(8,128)(2,1)S(1)} collective-permute-done((bf16[768,512]{1,0:T(8,128)(2,1)S(1)}, bf16[768,512]{1,0:T(8,128)(2,1)S(1)}, u32[]{:S(2)}, u32[]{:S(2)}) %collective-permute-start) | collective-permute-done | bytes 786464 | tf_op jit(solution)/shard_map/ppermute | solution.py:389
  27.5 0.7 sum_ma.1.refs_0_
  28.2 2.0 %make_h3_h2_h10.1 = (bf16[768,512]{1,0:T(8,128)(2,1)S(1)}, bf16[768,512]{1,0:T(8,128)(2,1)S(1)}, bf16[2,768,512]{2,1,0:T(8,128)(2,1)S(1)}) custom-call(s32[23]{0:T(128)S(1)} %get-tuple-element.16.flags, bf16[1024,768]{1,0:T(8,128)(2,1)} %hidden.7, bf16[1024,2048]{1,0:T(8,128)(2,1)} %grad.7, bf16[768,512]{1,0:T(8,128)(2,1)S(1)} %sum_ma.1.refs_0_), custom_call_target="tpu_custom_call" | custom-call | flops 1 | bytes 1 | tf_op jit(solution)/shard_map/make_h3_h2_h10/pallas_call | solution.py:332
  30.2 6.5 %collective-permute-start.5 = (bf16[768,512]{1,0:T(8,128)(2,1)S(1)}, bf16[768,512]{1,0:T(8,128)(2,1)S(1)}, u32[]{:S(2)}, u32[]{:S(2)}) collective-permute-start(bf16[768,512]{1,0:T(8,128)(2,1)S(1)} %sum_ma.1.refs_0_), channel_id=1, source_target_pairs={{8,16},{16,8},{9,17},{17,9},{10,18},{18,10},{11,19},{19,11},{12,20... | collective-permute-start | bytes 2359304 | tf_op jit(solution)/shard_map/ppermute | solution.py:392
  36.7 0.8 sum_s2.1.refs_3_
  37.5 1.4 %collective-permute-start.4 = (bf16[768,512]{1,0:T(8,128)(2,1)S(1)}, bf16[768,512]{1,0:T(8,128)(2,1)S(1)}, u32[]{:S(2)}, u32[]{:S(2)}) collective-permute-start(bf16[768,512]{1,0:T(8,128)(2,1)S(1)} %sum_s2.1.refs_3_), channel_id=1, source_target_pairs={{0,4},{1,3},{2,6},{3,1},{4,0},{5,7},{6,2},{7,5},{8,12},{9,11},{10,... | collective-permute-start | bytes 2359304 | tf_op jit(solution)/shard_map/ppermute | solution.py:386
  38.9 0.4 collective-permute-start.9
  39.2 0.9 sum_g3.1.refs_2_.refs_0_
  40.1 1.3 %collective-permute-start.8 = (bf16[768,512]{1,0:T(8,128)(2,1)S(1)}, bf16[768,512]{1,0:T(8,128)(2,1)S(1)}, u32[]{:S(2)}, u32[]{:S(2)}) collective-permute-start(bf16[768,512]{1,0:T(8,128)(2,1)S(1)} %sum_g3.1.refs_2_.refs_0_), channel_id=1, source_target_pairs={{0,8},{24,16},{1,9},{25,17},{2,10},{26,18},{3,11},{27,19},{4,12},{... | collective-permute-start | bytes 2359304 | tf_op jit(solution)/shard_map/ppermute | solution.py:389
  41.4 1.6 %collective-permute-done.6.refs_1_ = bf16[768,512]{1,0:T(8,128)(2,1)S(1)} collective-permute-done((bf16[768,512]{1,0:T(8,128)(2,1)S(1)}, bf16[768,512]{1,0:T(8,128)(2,1)S(1)}, u32[]{:S(2)}, u32[]{:S(2)}) %collective-permute-start.6) | collective-permute-done | bytes 786464 | tf_op jit(solution)/shard_map/ppermute | solution.py:389
  43.0 1.4 %collective-permute-start.2 = (bf16[768,512]{1,0:T(8,128)(2,1)S(1)}, bf16[768,512]{1,0:T(8,128)(2,1)S(1)}, u32[]{:S(2)}, u32[]{:S(2)}) collective-permute-start(bf16[768,512]{1,0:T(8,128)(2,1)S(1)} %get-tuple-element.22.refs_0_), channel_id=1, source_target_pairs={{0,2},{1,5},{2,0},{3,7},{4,6},{5,1},{6,4},{7,3},{8,10},{9,13},{10,... | collective-permute-start | bytes 2359304 | tf_op jit(solution)/shard_map/ppermute | solution.py:386
  44.4 0.7 sum_mb.1.refs_2_
  45.2 7.2 %collective-permute-done.5.refs_1_ = bf16[768,512]{1,0:T(8,128)(2,1)S(1)} collective-permute-done((bf16[768,512]{1,0:T(8,128)(2,1)S(1)}, bf16[768,512]{1,0:T(8,128)(2,1)S(1)}, u32[]{:S(2)}, u32[]{:S(2)}) %collective-permute-start.5) | collective-permute-done | bytes 786464 | tf_op jit(solution)/shard_map/ppermute | solution.py:392
  52.4 3.6 %collective-permute-start.12 = (bf16[768,512]{1,0:T(8,128)(2,1)S(1)}, bf16[768,512]{1,0:T(8,128)(2,1)S(1)}, u32[]{:S(2)}, u32[]{:S(2)}) collective-permute-start(bf16[768,512]{1,0:T(8,128)(2,1)S(1)} %sum_mb.1.refs_2_), channel_id=1, source_target_pairs={{8,16},{16,8},{9,17},{17,9},{10,18},{18,10},{11,19},{19,11},{12,20... | collective-permute-start | bytes 2359304 | tf_op jit(solution)/shard_map/ppermute | solution.py:392
  56.0 0.7 sum_xc.1.refs_3_
  56.7 1.3 %collective-permute-done.4.refs_2_ = bf16[768,512]{1,0:T(8,128)(2,1)S(1)} collective-permute-done((bf16[768,512]{1,0:T(8,128)(2,1)S(1)}, bf16[768,512]{1,0:T(8,128)(2,1)S(1)}, u32[]{:S(2)}, u32[]{:S(2)}) %collective-permute-start.4) | collective-permute-done | bytes 786464 | tf_op jit(solution)/shard_map/ppermute | solution.py:386
  58.0 0.9 sum_g2.1.refs_2_.refs_0_
  58.9 1.3 %collective-permute-start.11 = (bf16[768,512]{1,0:T(8,128)(2,1)S(1)}, bf16[768,512]{1,0:T(8,128)(2,1)S(1)}, u32[]{:S(2)}, u32[]{:S(2)}) collective-permute-start(bf16[768,512]{1,0:T(8,128)(2,1)S(1)} %sum_g2.1.refs_2_.refs_0_), channel_id=1, source_target_pairs={{0,8},{24,16},{1,9},{25,17},{2,10},{26,18},{3,11},{27,19},{4,12},{... | collective-permute-start | bytes 2359304 | tf_op jit(solution)/shard_map/ppermute | solution.py:389
  60.2 0.8 sum_s1.1.refs_2_
  61.0 1.4 %collective-permute-start.15 = (bf16[768,512]{1,0:T(8,128)(2,1)S(1)}, bf16[768,512]{1,0:T(8,128)(2,1)S(1)}, u32[]{:S(2)}, u32[]{:S(2)}) collective-permute-start(bf16[768,512]{1,0:T(8,128)(2,1)S(1)} %sum_s1.1.refs_2_), channel_id=1, source_target_pairs={{0,4},{1,3},{2,6},{3,1},{4,0},{5,7},{6,2},{7,5},{8,12},{9,11},{10,... | collective-permute-start | bytes 2359304 | tf_op jit(solution)/shard_map/ppermute | solution.py:386
  62.4 0.7 sum_mx.1.refs_2_
  63.2 3.3 %collective-permute-start.16 = (bf16[768,512]{1,0:T(8,128)(2,1)S(1)}, bf16[768,512]{1,0:T(8,128)(2,1)S(1)}, u32[]{:S(2)}, u32[]{:S(2)}) collective-permute-start(bf16[768,512]{1,0:T(8,128)(2,1)S(1)} %sum_mx.1.refs_2_), channel_id=1, source_target_pairs={{8,16},{16,8},{9,17},{17,9},{10,18},{18,10},{11,19},{19,11},{12,20... | collective-permute-start | bytes 2359304 | tf_op jit(solution)/shard_map/ppermute | solution.py:392
  66.5 3.8 %collective-permute-start.14 = (bf16[768,512]{1,0:T(8,128)(2,1)S(1)}, bf16[768,512]{1,0:T(8,128)(2,1)S(1)}, u32[]{:S(2)}, u32[]{:S(2)}) collective-permute-start(bf16[768,512]{1,0:T(8,128)(2,1)S(1)} %sum_xc.1.refs_3_), channel_id=1, source_target_pairs={{0,8},{8,0},{16,24},{24,16},{1,9},{9,1},{17,25},{25,17},{2,10},{10... | collective-permute-start | bytes 2359304 | tf_op jit(solution)/shard_map/ppermute | solution.py:395
  70.3 0.8 sum_s0.1.refs_2_
  71.1 10.1 %collective-permute-done.11.refs_1_ = bf16[768,512]{1,0:T(8,128)(2,1)S(1)} collective-permute-done((bf16[768,512]{1,0:T(8,128)(2,1)S(1)}, bf16[768,512]{1,0:T(8,128)(2,1)S(1)}, u32[]{:S(2)}, u32[]{:S(2)}) %collective-permute-start.11) | collective-permute-done | bytes 786464 | tf_op jit(solution)/shard_map/ppermute | solution.py:389
  81.2 1.4 %collective-permute-start.10 = (bf16[768,512]{1,0:T(8,128)(2,1)S(1)}, bf16[768,512]{1,0:T(8,128)(2,1)S(1)}, u32[]{:S(2)}, u32[]{:S(2)}) collective-permute-start(bf16[768,512]{1,0:T(8,128)(2,1)S(1)} %sum_s0.1.refs_2_), channel_id=1, source_target_pairs={{0,4},{1,3},{2,6},{3,1},{4,0},{5,7},{6,2},{7,5},{8,12},{9,11},{10,... | collective-permute-start | bytes 2359304 | tf_op jit(solution)/shard_map/ppermute | solution.py:386
  82.6 0.7 sum_my.1.refs_4_
  83.3 4.0 %collective-permute-start.13 = (bf16[768,512]{1,0:T(8,128)(2,1)S(1)}, bf16[768,512]{1,0:T(8,128)(2,1)S(1)}, u32[]{:S(2)}, u32[]{:S(2)}) collective-permute-start(bf16[768,512]{1,0:T(8,128)(2,1)S(1)} %sum_my.1.refs_4_), channel_id=1, source_target_pairs={{8,16},{16,8},{9,17},{17,9},{10,18},{18,10},{11,19},{19,11},{12,20... | collective-permute-start | bytes 2359304 | tf_op jit(solution)/shard_map/ppermute | solution.py:392
  87.4 3.6 %collective-permute-done.16.refs_3_ = bf16[768,512]{1,0:T(8,128)(2,1)S(1)} collective-permute-done((bf16[768,512]{1,0:T(8,128)(2,1)S(1)}, bf16[768,512]{1,0:T(8,128)(2,1)S(1)}, u32[]{:S(2)}, u32[]{:S(2)}) %collective-permute-start.16) | collective-permute-done | bytes 786464 | tf_op jit(solution)/shard_map/ppermute | solution.py:392
  91.0 1.0 sum_xh.1.refs_3_
  92.0 0.1 collective-permute-start.17
  92.1 6.0 %collective-permute-done.14.refs_2_ = bf16[768,512]{1,0:T(8,128)(2,1)S(1)} collective-permute-done((bf16[768,512]{1,0:T(8,128)(2,1)S(1)}, bf16[768,512]{1,0:T(8,128)(2,1)S(1)}, u32[]{:S(2)}, u32[]{:S(2)}) %collective-permute-start.14) | collective-permute-done | bytes 786464 | tf_op jit(solution)/shard_map/ppermute | solution.py:395
  98.1 1.5 %sum_f.1.refs_4_.refs_2_ = bf16[2,768,512]{2,1,0:T(8,128)(2,1)} custom-call(s32[23]{0:T(128)S(1)} %get-tuple-element.16.flags, bf16[3,768,512]{2,1,0:T(8,128)(2,1)S(1)} %get-tuple-element.25.refs_0_, bf16[768,512]{1,0:T(8,128)(2,1)S(1)} %collective-permute-done.12.refs_3_.refs_1_, bf16[768,512]{1,0:T(8,128)(2,1)S(1)} %collective-permute-done.14.refs_2_, ...), custom_call_target="tpu_custom_call" | custom-call | flops 1 | bytes 1 | tf_op jit(solution)/shard_map/sum_f/pallas_call | solution.py:362
  99.6 5.1 %collective-permute-done.13.refs_3_ = bf16[768,512]{1,0:T(8,128)(2,1)S(1)} collective-permute-done((bf16[768,512]{1,0:T(8,128)(2,1)S(1)}, bf16[768,512]{1,0:T(8,128)(2,1)S(1)}, u32[]{:S(2)}, u32[]{:S(2)}) %collective-permute-start.13) | collective-permute-done | bytes 786464 | tf_op jit(solution)/shard_map/ppermute | solution.py:392
  104.8 1.4 %copy-done = bf16[2,768,512]{2,1,0:T(8,128)(2,1)S(1)} copy-done((bf16[2,768,512]{2,1,0:T(8,128)(2,1)S(1)}, bf16[2,768,512]{2,1,0:T(8,128)(2,1)}, u32[]{:S(2)}) %copy-start) | copy-done | bytes 1572888
  106.2 1.0 sum_g0.1.refs_0_
  107.1 5.1 %collective-permute-done.17.refs_1_ = bf16[768,512]{1,0:T(8,128)(2,1)S(1)} collective-permute-done((bf16[768,512]{1,0:T(8,128)(2,1)S(1)}, bf16[768,512]{1,0:T(8,128)(2,1)S(1)}, u32[]{:S(2)}, u32[]{:S(2)}) %collective-permute-start.17) | collective-permute-done | bytes 786464 | tf_op jit(solution)/shard_map/ppermute | solution.py:395
  112.3 1.5 %finish.1 = bf16[2,768,512]{2,1,0:T(8,128)(2,1)} custom-call(s32[23]{0:T(128)S(1)} %get-tuple-element.16.flags, bf16[768,512]{1,0:T(8,128)(2,1)S(1)} %sum_g0.1.refs_0_, bf16[768,512]{1,0:T(8,128)(2,1)S(1)} %collective-permute-done.17.refs_1_, bf16[2,768,512]{2,1,0:T(8,128)(2,1)} %sum_f.1.refs_4_.refs_2_), custom_call_target="tpu_custom_call", output_to_operand_aliasing={{}: (3, {})} | custom-call | flops 1 | bytes 1 | tf_op jit(solution)/shard_map/finish/pallas_call | solution.py:362
  (9 shorter events, 0.0 us)
Async XLA Ops:
  3.7 12.1 %collective-permute-start.1 = (bf16[768,512]{1,0:T(8,128)(2,1)S(1)}, bf16[768,512]{1,0:T(8,128)(2,1)S(1)}, u32[]{:S(2)}, u32[]{:S(2)}) collective-permute-start(bf16[768,512]{1,0:T(8,128)(2,1)S(1)} %get-tuple-element.19.refs_0_), channel_id=1, source_target_pairs={{0,2},{1,5},{2,0},{3,7},{4,6},{5,1},{6,4},{7,3},{8,10},{9,13},{10,... | collective-permute-start | bytes 2359304 | tf_op jit(solution)/shard_map/ppermute | solution.py:386
  5.3 22.2 %collective-permute-start = (bf16[768,512]{1,0:T(8,128)(2,1)S(1)}, bf16[768,512]{1,0:T(8,128)(2,1)S(1)}, u32[]{:S(2)}, u32[]{:S(2)}) collective-permute-start(bf16[768,512]{1,0:T(8,128)(2,1)S(1)} %get-tuple-element.17.refs_0_), channel_id=1, source_target_pairs={{0,8},{24,16},{1,9},{25,17},{2,10},{26,18},{3,11},{27,19},{4,12},{... | collective-permute-start | bytes 2359304 | tf_op jit(solution)/shard_map/ppermute | solution.py:389
  14.6 22.1 %collective-permute-start.3 = (bf16[768,512]{1,0:T(8,128)(2,1)S(1)}, bf16[768,512]{1,0:T(8,128)(2,1)S(1)}, u32[]{:S(2)}, u32[]{:S(2)}) collective-permute-start(bf16[768,512]{1,0:T(8,128)(2,1)S(1)} %get-tuple-element.20.refs_2_.refs_0_), channel_id=1, source_target_pairs={{0,2},{1,5},{2,0},{3,7},{4,6},{5,1},{6,4},{7,3},{8,10},{9,13},{10,... | collective-permute-start | bytes 2359304 | tf_op jit(solution)/shard_map/ppermute | solution.py:386
  16.6 22.7 %collective-permute-start.7 = (bf16[768,512]{1,0:T(8,128)(2,1)S(1)}, bf16[768,512]{1,0:T(8,128)(2,1)S(1)}, u32[]{:S(2)}, u32[]{:S(2)}) collective-permute-start(bf16[768,512]{1,0:T(8,128)(2,1)S(1)} %sum_s3.1.refs_2_), channel_id=1, source_target_pairs={{0,4},{1,3},{2,6},{3,1},{4,0},{5,7},{6,2},{7,5},{8,12},{9,11},{10,... | collective-permute-start | bytes 2359304 | tf_op jit(solution)/shard_map/ppermute | solution.py:386
  19.1 23.9 %collective-permute-start.6 = (bf16[768,512]{1,0:T(8,128)(2,1)S(1)}, bf16[768,512]{1,0:T(8,128)(2,1)S(1)}, u32[]{:S(2)}, u32[]{:S(2)}) collective-permute-start(bf16[768,512]{1,0:T(8,128)(2,1)S(1)} %get-tuple-element.18.refs_0_), channel_id=1, source_target_pairs={{0,8},{24,16},{1,9},{25,17},{2,10},{26,18},{3,11},{27,19},{4,12},{... | collective-permute-start | bytes 2359304 | tf_op jit(solution)/shard_map/ppermute | solution.py:389
  30.2 22.2 %collective-permute-start.5 = (bf16[768,512]{1,0:T(8,128)(2,1)S(1)}, bf16[768,512]{1,0:T(8,128)(2,1)S(1)}, u32[]{:S(2)}, u32[]{:S(2)}) collective-permute-start(bf16[768,512]{1,0:T(8,128)(2,1)S(1)} %sum_ma.1.refs_0_), channel_id=1, source_target_pairs={{8,16},{16,8},{9,17},{17,9},{10,18},{18,10},{11,19},{19,11},{12,20... | collective-permute-start | bytes 2359304 | tf_op jit(solution)/shard_map/ppermute | solution.py:392
  37.5 20.5 %collective-permute-start.4 = (bf16[768,512]{1,0:T(8,128)(2,1)S(1)}, bf16[768,512]{1,0:T(8,128)(2,1)S(1)}, u32[]{:S(2)}, u32[]{:S(2)}) collective-permute-start(bf16[768,512]{1,0:T(8,128)(2,1)S(1)} %sum_s2.1.refs_3_), channel_id=1, source_target_pairs={{0,4},{1,3},{2,6},{3,1},{4,0},{5,7},{6,2},{7,5},{8,12},{9,11},{10,... | collective-permute-start | bytes 2359304 | tf_op jit(solution)/shard_map/ppermute | solution.py:386
  38.9 21.3 %collective-permute-start.9 = (bf16[768,512]{1,0:T(8,128)(2,1)S(1)}, bf16[768,512]{1,0:T(8,128)(2,1)S(1)}, u32[]{:S(2)}, u32[]{:S(2)}) collective-permute-start(bf16[768,512]{1,0:T(8,128)(2,1)S(1)} %get-tuple-element.26.refs_0_), channel_id=1, source_target_pairs={{0,2},{1,5},{2,0},{3,7},{4,6},{5,1},{6,4},{7,3},{8,10},{9,13},{10,... | collective-permute-start | bytes 2359304 | tf_op jit(solution)/shard_map/ppermute | solution.py:386
  40.1 22.3 %collective-permute-start.8 = (bf16[768,512]{1,0:T(8,128)(2,1)S(1)}, bf16[768,512]{1,0:T(8,128)(2,1)S(1)}, u32[]{:S(2)}, u32[]{:S(2)}) collective-permute-start(bf16[768,512]{1,0:T(8,128)(2,1)S(1)} %sum_g3.1.refs_2_.refs_0_), channel_id=1, source_target_pairs={{0,8},{24,16},{1,9},{25,17},{2,10},{26,18},{3,11},{27,19},{4,12},{... | collective-permute-start | bytes 2359304 | tf_op jit(solution)/shard_map/ppermute | solution.py:389
  43.0 23.5 %collective-permute-start.2 = (bf16[768,512]{1,0:T(8,128)(2,1)S(1)}, bf16[768,512]{1,0:T(8,128)(2,1)S(1)}, u32[]{:S(2)}, u32[]{:S(2)}) collective-permute-start(bf16[768,512]{1,0:T(8,128)(2,1)S(1)} %get-tuple-element.22.refs_0_), channel_id=1, source_target_pairs={{0,2},{1,5},{2,0},{3,7},{4,6},{5,1},{6,4},{7,3},{8,10},{9,13},{10,... | collective-permute-start | bytes 2359304 | tf_op jit(solution)/shard_map/ppermute | solution.py:386
  52.4 30.2 %collective-permute-start.12 = (bf16[768,512]{1,0:T(8,128)(2,1)S(1)}, bf16[768,512]{1,0:T(8,128)(2,1)S(1)}, u32[]{:S(2)}, u32[]{:S(2)}) collective-permute-start(bf16[768,512]{1,0:T(8,128)(2,1)S(1)} %sum_mb.1.refs_2_), channel_id=1, source_target_pairs={{8,16},{16,8},{9,17},{17,9},{10,18},{18,10},{11,19},{19,11},{12,20... | collective-permute-start | bytes 2359304 | tf_op jit(solution)/shard_map/ppermute | solution.py:392
  58.9 22.4 %collective-permute-start.11 = (bf16[768,512]{1,0:T(8,128)(2,1)S(1)}, bf16[768,512]{1,0:T(8,128)(2,1)S(1)}, u32[]{:S(2)}, u32[]{:S(2)}) collective-permute-start(bf16[768,512]{1,0:T(8,128)(2,1)S(1)} %sum_g2.1.refs_2_.refs_0_), channel_id=1, source_target_pairs={{0,8},{24,16},{1,9},{25,17},{2,10},{26,18},{3,11},{27,19},{4,12},{... | collective-permute-start | bytes 2359304 | tf_op jit(solution)/shard_map/ppermute | solution.py:389
  61.0 26.3 %collective-permute-start.15 = (bf16[768,512]{1,0:T(8,128)(2,1)S(1)}, bf16[768,512]{1,0:T(8,128)(2,1)S(1)}, u32[]{:S(2)}, u32[]{:S(2)}) collective-permute-start(bf16[768,512]{1,0:T(8,128)(2,1)S(1)} %sum_s1.1.refs_2_), channel_id=1, source_target_pairs={{0,4},{1,3},{2,6},{3,1},{4,0},{5,7},{6,2},{7,5},{8,12},{9,11},{10,... | collective-permute-start | bytes 2359304 | tf_op jit(solution)/shard_map/ppermute | solution.py:386
  63.2 27.8 %collective-permute-start.16 = (bf16[768,512]{1,0:T(8,128)(2,1)S(1)}, bf16[768,512]{1,0:T(8,128)(2,1)S(1)}, u32[]{:S(2)}, u32[]{:S(2)}) collective-permute-start(bf16[768,512]{1,0:T(8,128)(2,1)S(1)} %sum_mx.1.refs_2_), channel_id=1, source_target_pairs={{8,16},{16,8},{9,17},{17,9},{10,18},{18,10},{11,19},{19,11},{12,20... | collective-permute-start | bytes 2359304 | tf_op jit(solution)/shard_map/ppermute | solution.py:392
  66.5 31.6 %collective-permute-start.14 = (bf16[768,512]{1,0:T(8,128)(2,1)S(1)}, bf16[768,512]{1,0:T(8,128)(2,1)S(1)}, u32[]{:S(2)}, u32[]{:S(2)}) collective-permute-start(bf16[768,512]{1,0:T(8,128)(2,1)S(1)} %sum_xc.1.refs_3_), channel_id=1, source_target_pairs={{0,8},{8,0},{16,24},{24,16},{1,9},{9,1},{17,25},{25,17},{2,10},{10... | collective-permute-start | bytes 2359304 | tf_op jit(solution)/shard_map/ppermute | solution.py:395
  81.2 23.5 %collective-permute-start.10 = (bf16[768,512]{1,0:T(8,128)(2,1)S(1)}, bf16[768,512]{1,0:T(8,128)(2,1)S(1)}, u32[]{:S(2)}, u32[]{:S(2)}) collective-permute-start(bf16[768,512]{1,0:T(8,128)(2,1)S(1)} %sum_s0.1.refs_2_), channel_id=1, source_target_pairs={{0,4},{1,3},{2,6},{3,1},{4,0},{5,7},{6,2},{7,5},{8,12},{9,11},{10,... | collective-permute-start | bytes 2359304 | tf_op jit(solution)/shard_map/ppermute | solution.py:386
  83.3 21.4 %collective-permute-start.13 = (bf16[768,512]{1,0:T(8,128)(2,1)S(1)}, bf16[768,512]{1,0:T(8,128)(2,1)S(1)}, u32[]{:S(2)}, u32[]{:S(2)}) collective-permute-start(bf16[768,512]{1,0:T(8,128)(2,1)S(1)} %sum_my.1.refs_4_), channel_id=1, source_target_pairs={{8,16},{16,8},{9,17},{17,9},{10,18},{18,10},{11,19},{19,11},{12,20... | collective-permute-start | bytes 2359304 | tf_op jit(solution)/shard_map/ppermute | solution.py:392
  92.0 20.3 %collective-permute-start.17 = (bf16[768,512]{1,0:T(8,128)(2,1)S(1)}, bf16[768,512]{1,0:T(8,128)(2,1)S(1)}, u32[]{:S(2)}, u32[]{:S(2)}) collective-permute-start(bf16[768,512]{1,0:T(8,128)(2,1)S(1)} %sum_xh.1.refs_3_), channel_id=1, source_target_pairs={{0,8},{8,0},{16,24},{24,16},{1,9},{9,1},{17,25},{25,17},{2,10},{10... | collective-permute-start | bytes 2359304 | tf_op jit(solution)/shard_map/ppermute | solution.py:395
  104.8 1.4 %copy-start = (bf16[2,768,512]{2,1,0:T(8,128)(2,1)S(1)}, bf16[2,768,512]{2,1,0:T(8,128)(2,1)}, u32[]{:S(2)}) copy-start(bf16[2,768,512]{2,1,0:T(8,128)(2,1)} %sum_f.1.refs_4_.refs_2_) | copy-start | bytes 4718596

commit v3 on v2

--- a/solution.py
+++ b/solution.py
@@ -8,7 +8,7 @@
 from jax.sharding import PartitionSpec as P
 
 EXP_DEV = 2
-ORDER = ("c3,r3", "c2,c103", "r2,r1,r0", "s3", "ma", "h3,h2,h10", "s2", "g3", "mb", "xc", "g2", "s1", "mx", "s0", "my@mb", "xh", "f", "g0")
+ORDER = ("c3,r3", "c2,c10", "r2,r1,r0", "s3", "ma", "h3,h2,h10", "s2", "g3", "mb", "xc", "g2", "s1", "mx", "s0", "my@mb", "xh", "f", "g0")
 COLD, HOT, REPLICA = 0, 1, 2
 SMEM = pl.BlockSpec(memory_space=pltpu.SMEM)
 VMEM = pl.BlockSpec(memory_space=pltpu.VMEM)
@@ -178,9 +178,6 @@
         copy.wait()
     for (kind, _), out in zip(found, outs):
         count = flags[blocks + F_BLOCKS + kind]
-        if kind == COLD:
-            here, n = lax.axis_index("dp"), lax.axis_size("dp")
-            count = jnp.where((here == 0) | (here == n - 1), count, 0)
 
         @pl.when(count == 0)
         def _(out=out):

time: 115 us -> 114 us (level)
  starting transfers between devices: 36.9 us -> 31.8 us
  Pallas kernels: 26.7 us -> 31 us
    ppermute x4, waiting for transfers between devices: 15.9 us -> 0.29 us  [middle(): return lax.ppermute(x, 'dp', [(1, 2), (2, 1)])]
    ppermute x8, waiting for transfers between devices: 2.03 us -> 11.4 us  [plane(): return lax.ppermute(x, 'expert', pairs)]
    ppermute x2, waiting for transfers between devices: 11.2 us -> 17.8 us  [both(): return lax.ppermute(x, 'dp', [(0, 1), (1, 0), (2, 3), (3, 2)])]
    ppermute x4, starting transfers between devices: 17.4 us -> 11.6 us  [middle(): return lax.ppermute(x, 'dp', [(1, 2), (2, 1)])]
    pallas_call x3, Pallas kernels: 10 us -> 13.3 us  [product(): pl.pallas_call(functools.partial(product_kernel, groups, blocks), out_sha...]
    ppermute x8, starting transfers between devices: 10.4 us -> 13.3 us  [plane(): return lax.ppermute(x, 'expert', pairs)]
    ppermute x2, starting transfers between devices: 3.84 us -> 1.82 us  [both(): return lax.ppermute(x, 'dp', [(0, 1), (1, 0), (2, 3), (3, 2)])]
  transfers between devices with their start and end apart: 18 -> 18, of which waited for: 10 -> 8; matrix products, arithmetic and copies ran while one was open for 0% -> 0% of each run, Pallas kernels for 19% -> 23%
where the time goes in v3:
time: 114 us; the launch traced here: 113 us
  waiting for transfers between devices  47.4 us (42%)
  starting transfers between devices  31.8 us (28%)
  Pallas kernels  31 us (27%)
  local copies, waits for them, and re-layouts  1.4 us (1%)
    ppermute x4, waiting for transfers between devices, outer(): return lax.ppermute(x, 'dp', [(0, 1), (n - 1, n - 2)])  17.9 us
    ppermute x2, waiting for transfers between devices, both(): return lax.ppermute(x, 'dp', [(0, 1), (1, 0), (2, 3), (3, 2)])  17.8 us
    pallas_call x3, Pallas kernels, product(): pl.pallas_call(functools.partial(product_kernel, groups, blocks), out_sha...  13.3 us
    ppermute x8, starting transfers between devices, plane(): return lax.ppermute(x, 'expert', pairs)  13.3 us
    ppermute x4, starting transfers between devices, middle(): return lax.ppermute(x, 'dp', [(1, 2), (2, 1)])  11.6 us
    ppermute x8, waiting for transfers between devices, plane(): return lax.ppermute(x, 'expert', pairs)  11.4 us
    pallas_call x13, Pallas kernels, combine(): pl.pallas_call(functools.partial(combine_kernel, groups, blocks, len(arra...  10.6 us
    ppermute x4, starting transfers between devices, outer(): return lax.ppermute(x, 'dp', [(0, 1), (n - 1, n - 2)])  5.14 us
  transfers between devices with their start and end apart: 18, of which 8 were waited for; matrix products, arithmetic and copies ran while one was open for 0% of the time, Pallas kernels for 23%

profile of v3, /device:TPU:8, one launch (start us, length us, event | category | flops | bytes accessed | tf_op | source)
XLA Modules:
  0.0 112.5 jit_solution(13375283560831610248)
XLA Ops:
  0.7 4.1 %open_c3_r3.1 = (s32[23]{0:T(128)S(1)}, bf16[768,512]{1,0:T(8,128)(2,1)S(1)}, bf16[768,512]{1,0:T(8,128)(2,1)S(1)}) custom-call(s32[1,8]{1,0:T(1,128)} %slots.1, s32[1]{0:T(128)S(6)} %copy.8.counts, s32[8]{0:T(128)} %placement.1, bf16[1024,768]{1,0:T(8,128)(2,1)} %hidden.7, bf16[1024,2048]{1,0:T(8,128)(2,1)} %grad.7), custom_call_target="tpu_custom_call" | custom-call | flops 1 | bytes 1 | tf_op jit(solution)/shard_map/open_c3_r3/pallas_call | solution.py:305
  4.8 1.5 %collective-permute-start.1 = (bf16[768,512]{1,0:T(8,128)(2,1)S(1)}, bf16[768,512]{1,0:T(8,128)(2,1)S(1)}, u32[]{:S(2)}, u32[]{:S(2)}) collective-permute-start(bf16[768,512]{1,0:T(8,128)(2,1)S(1)} %get-tuple-element.19.refs_0_), channel_id=1, source_target_pairs={{0,2},{1,5},{2,0},{3,7},{4,6},{5,1},{6,4},{7,3},{8,10},{9,13},{10,... | collective-permute-start | bytes 2359304 | tf_op jit(solution)/shard_map/ppermute | solution.py:383
  6.2 1.3 %collective-permute-start = (bf16[768,512]{1,0:T(8,128)(2,1)S(1)}, bf16[768,512]{1,0:T(8,128)(2,1)S(1)}, u32[]{:S(2)}, u32[]{:S(2)}) collective-permute-start(bf16[768,512]{1,0:T(8,128)(2,1)S(1)} %get-tuple-element.17.refs_0_), channel_id=1, source_target_pairs={{0,8},{24,16},{1,9},{25,17},{2,10},{26,18},{3,11},{27,19},{4,12},{... | collective-permute-start | bytes 2359304 | tf_op jit(solution)/shard_map/ppermute | solution.py:386
  7.5 3.5 %make_c2_c10.1 = (bf16[768,512]{1,0:T(8,128)(2,1)S(1)}, bf16[2,768,512]{2,1,0:T(8,128)(2,1)S(1)}) custom-call(s32[23]{0:T(128)S(1)} %get-tuple-element.16.flags, bf16[1024,768]{1,0:T(8,128)(2,1)} %hidden.7, bf16[1024,2048]{1,0:T(8,128)(2,1)} %grad.7, bf16[768,512]{1,0:T(8,128)(2,1)S(1)} %get-tuple-element.17.refs_0_), custom_call_target="tpu_custom_call" | custom-call | flops 1 | bytes 1 | tf_op jit(solution)/shard_map/make_c2_c10/pallas_call | solution.py:329
  11.1 5.3 %make_r2_r1_r0.1 = (bf16[768,512]{1,0:T(8,128)(2,1)S(1)}, bf16[768,512]{1,0:T(8,128)(2,1)S(1)}, bf16[768,512]{1,0:T(8,128)(2,1)S(1)}) custom-call(s32[23]{0:T(128)S(1)} %get-tuple-element.16.flags, bf16[1024,768]{1,0:T(8,128)(2,1)} %hidden.7, bf16[1024,2048]{1,0:T(8,128)(2,1)} %grad.7, bf16[768,512]{1,0:T(8,128)(2,1)S(1)} %get-tuple-element.18.refs_0_), custom_call_target="tpu_custom_call" | custom-call | flops 1 | bytes 1 | tf_op jit(solution)/shard_map/make_r2_r1_r0/pallas_call | solution.py:329
  16.4 0.5 collective-permute-start.3
  17.0 0.8 sum_s3.1.refs_2_
  17.8 3.4 %collective-permute-start.7 = (bf16[768,512]{1,0:T(8,128)(2,1)S(1)}, bf16[768,512]{1,0:T(8,128)(2,1)S(1)}, u32[]{:S(2)}, u32[]{:S(2)}) collective-permute-start(bf16[768,512]{1,0:T(8,128)(2,1)S(1)} %sum_s3.1.refs_2_), channel_id=1, source_target_pairs={{0,4},{1,3},{2,6},{3,1},{4,0},{5,7},{6,2},{7,5},{8,12},{9,11},{10,... | collective-permute-start | bytes 2359304 | tf_op jit(solution)/shard_map/ppermute | solution.py:383
  21.2 1.3 %collective-permute-start.6 = (bf16[768,512]{1,0:T(8,128)(2,1)S(1)}, bf16[768,512]{1,0:T(8,128)(2,1)S(1)}, u32[]{:S(2)}, u32[]{:S(2)}) collective-permute-start(bf16[768,512]{1,0:T(8,128)(2,1)S(1)} %get-tuple-element.18.refs_0_), channel_id=1, source_target_pairs={{0,8},{24,16},{1,9},{25,17},{2,10},{26,18},{3,11},{27,19},{4,12},{... | collective-permute-start | bytes 2359304 | tf_op jit(solution)/shard_map/ppermute | solution.py:386
  22.5 6.1 %collective-permute-done.refs_1_ = bf16[768,512]{1,0:T(8,128)(2,1)S(1)} collective-permute-done((bf16[768,512]{1,0:T(8,128)(2,1)S(1)}, bf16[768,512]{1,0:T(8,128)(2,1)S(1)}, u32[]{:S(2)}, u32[]{:S(2)}) %collective-permute-start) | collective-permute-done | bytes 786464 | tf_op jit(solution)/shard_map/ppermute | solution.py:386
  28.6 0.7 sum_ma.1.refs_0_
  29.3 4.1 %collective-permute-start.5 = (bf16[768,512]{1,0:T(8,128)(2,1)S(1)}, bf16[768,512]{1,0:T(8,128)(2,1)S(1)}, u32[]{:S(2)}, u32[]{:S(2)}) collective-permute-start(bf16[768,512]{1,0:T(8,128)(2,1)S(1)} %sum_ma.1.refs_0_), channel_id=1, source_target_pairs={{8,16},{16,8},{9,17},{17,9},{10,18},{18,10},{11,19},{19,11},{12,20... | collective-permute-start | bytes 2359304 | tf_op jit(solution)/shard_map/ppermute | solution.py:389
  33.5 4.4 %make_h3_h2_h10.1 = (bf16[768,512]{1,0:T(8,128)(2,1)S(1)}, bf16[768,512]{1,0:T(8,128)(2,1)S(1)}, bf16[2,768,512]{2,1,0:T(8,128)(2,1)S(1)}) custom-call(s32[23]{0:T(128)S(1)} %get-tuple-element.16.flags, bf16[1024,768]{1,0:T(8,128)(2,1)} %hidden.7, bf16[1024,2048]{1,0:T(8,128)(2,1)} %grad.7, bf16[768,512]{1,0:T(8,128)(2,1)S(1)} %sum_ma.1.refs_0_), custom_call_target="tpu_custom_call" | custom-call | flops 1 | bytes 1 | tf_op jit(solution)/shard_map/make_h3_h2_h10/pallas_call | solution.py:329
  37.9 0.0 collective-permute-done.3.refs_1_
  37.9 0.8 sum_s2.1.refs_3_
  38.7 3.1 %collective-permute-start.4 = (bf16[768,512]{1,0:T(8,128)(2,1)S(1)}, bf16[768,512]{1,0:T(8,128)(2,1)S(1)}, u32[]{:S(2)}, u32[]{:S(2)}) collective-permute-start(bf16[768,512]{1,0:T(8,128)(2,1)S(1)} %sum_s2.1.refs_3_), channel_id=1, source_target_pairs={{0,4},{1,3},{2,6},{3,1},{4,0},{5,7},{6,2},{7,5},{8,12},{9,11},{10,... | collective-permute-start | bytes 2359304 | tf_op jit(solution)/shard_map/ppermute | solution.py:383
  41.8 0.0 collective-permute-start.9
  41.8 0.9 sum_g3.1.refs_2_.refs_0_
  42.7 1.3 %collective-permute-start.8 = (bf16[768,512]{1,0:T(8,128)(2,1)S(1)}, bf16[768,512]{1,0:T(8,128)(2,1)S(1)}, u32[]{:S(2)}, u32[]{:S(2)}) collective-permute-start(bf16[768,512]{1,0:T(8,128)(2,1)S(1)} %sum_g3.1.refs_2_.refs_0_), channel_id=1, source_target_pairs={{0,8},{24,16},{1,9},{25,17},{2,10},{26,18},{3,11},{27,19},{4,12},{... | collective-permute-start | bytes 2359304 | tf_op jit(solution)/shard_map/ppermute | solution.py:386
  44.0 1.5 %collective-permute-done.6.refs_1_ = bf16[768,512]{1,0:T(8,128)(2,1)S(1)} collective-permute-done((bf16[768,512]{1,0:T(8,128)(2,1)S(1)}, bf16[768,512]{1,0:T(8,128)(2,1)S(1)}, u32[]{:S(2)}, u32[]{:S(2)}) %collective-permute-start.6) | collective-permute-done | bytes 786464 | tf_op jit(solution)/shard_map/ppermute | solution.py:386
  45.5 0.6 collective-permute-start.2
  46.1 0.7 sum_mb.1.refs_2_
  46.8 0.3 collective-permute-done.5.refs_1_
  47.1 3.6 %collective-permute-start.12 = (bf16[768,512]{1,0:T(8,128)(2,1)S(1)}, bf16[768,512]{1,0:T(8,128)(2,1)S(1)}, u32[]{:S(2)}, u32[]{:S(2)}) collective-permute-start(bf16[768,512]{1,0:T(8,128)(2,1)S(1)} %sum_mb.1.refs_2_), channel_id=1, source_target_pairs={{8,16},{16,8},{9,17},{17,9},{10,18},{18,10},{11,19},{19,11},{12,20... | collective-permute-start | bytes 2359304 | tf_op jit(solution)/shard_map/ppermute | solution.py:389
  50.7 0.7 sum_xc.1.refs_3_
  51.5 8.8 %collective-permute-done.4.refs_2_ = bf16[768,512]{1,0:T(8,128)(2,1)S(1)} collective-permute-done((bf16[768,512]{1,0:T(8,128)(2,1)S(1)}, bf16[768,512]{1,0:T(8,128)(2,1)S(1)}, u32[]{:S(2)}, u32[]{:S(2)}) %collective-permute-start.4) | collective-permute-done | bytes 786464 | tf_op jit(solution)/shard_map/ppermute | solution.py:383
  60.2 0.9 sum_g2.1.refs_2_.refs_0_
  61.1 1.3 %collective-permute-start.11 = (bf16[768,512]{1,0:T(8,128)(2,1)S(1)}, bf16[768,512]{1,0:T(8,128)(2,1)S(1)}, u32[]{:S(2)}, u32[]{:S(2)}) collective-permute-start(bf16[768,512]{1,0:T(8,128)(2,1)S(1)} %sum_g2.1.refs_2_.refs_0_), channel_id=1, source_target_pairs={{0,8},{24,16},{1,9},{25,17},{2,10},{26,18},{3,11},{27,19},{4,12},{... | collective-permute-start | bytes 2359304 | tf_op jit(solution)/shard_map/ppermute | solution.py:386
  62.4 0.8 sum_s1.1.refs_2_
  63.3 2.1 %collective-permute-start.15 = (bf16[768,512]{1,0:T(8,128)(2,1)S(1)}, bf16[768,512]{1,0:T(8,128)(2,1)S(1)}, u32[]{:S(2)}, u32[]{:S(2)}) collective-permute-start(bf16[768,512]{1,0:T(8,128)(2,1)S(1)} %sum_s1.1.refs_2_), channel_id=1, source_target_pairs={{0,4},{1,3},{2,6},{3,1},{4,0},{5,7},{6,2},{7,5},{8,12},{9,11},{10,... | collective-permute-start | bytes 2359304 | tf_op jit(solution)/shard_map/ppermute | solution.py:383
  65.4 0.7 sum_mx.1.refs_2_
  66.1 1.9 %collective-permute-start.16 = (bf16[768,512]{1,0:T(8,128)(2,1)S(1)}, bf16[768,512]{1,0:T(8,128)(2,1)S(1)}, u32[]{:S(2)}, u32[]{:S(2)}) collective-permute-start(bf16[768,512]{1,0:T(8,128)(2,1)S(1)} %sum_mx.1.refs_2_), channel_id=1, source_target_pairs={{8,16},{16,8},{9,17},{17,9},{10,18},{18,10},{11,19},{19,11},{12,20... | collective-permute-start | bytes 2359304 | tf_op jit(solution)/shard_map/ppermute | solution.py:389
  68.0 2.6 %collective-permute-done.2.refs_1_ = bf16[768,512]{1,0:T(8,128)(2,1)S(1)} collective-permute-done((bf16[768,512]{1,0:T(8,128)(2,1)S(1)}, bf16[768,512]{1,0:T(8,128)(2,1)S(1)}, u32[]{:S(2)}, u32[]{:S(2)}) %collective-permute-start.2) | collective-permute-done | bytes 786464 | tf_op jit(solution)/shard_map/ppermute | solution.py:383
  70.6 1.8 %collective-permute-start.14 = (bf16[768,512]{1,0:T(8,128)(2,1)S(1)}, bf16[768,512]{1,0:T(8,128)(2,1)S(1)}, u32[]{:S(2)}, u32[]{:S(2)}) collective-permute-start(bf16[768,512]{1,0:T(8,128)(2,1)S(1)} %sum_xc.1.refs_3_), channel_id=1, source_target_pairs={{0,8},{8,0},{16,24},{24,16},{1,9},{9,1},{17,25},{25,17},{2,10},{10... | collective-permute-start | bytes 2359304 | tf_op jit(solution)/shard_map/ppermute | solution.py:392
  72.3 0.8 sum_s0.1.refs_2_
  73.2 10.3 %collective-permute-done.11.refs_1_ = bf16[768,512]{1,0:T(8,128)(2,1)S(1)} collective-permute-done((bf16[768,512]{1,0:T(8,128)(2,1)S(1)}, bf16[768,512]{1,0:T(8,128)(2,1)S(1)}, u32[]{:S(2)}, u32[]{:S(2)}) %collective-permute-start.11) | collective-permute-done | bytes 786464 | tf_op jit(solution)/shard_map/ppermute | solution.py:386
  83.5 2.0 %collective-permute-start.10 = (bf16[768,512]{1,0:T(8,128)(2,1)S(1)}, bf16[768,512]{1,0:T(8,128)(2,1)S(1)}, u32[]{:S(2)}, u32[]{:S(2)}) collective-permute-start(bf16[768,512]{1,0:T(8,128)(2,1)S(1)} %sum_s0.1.refs_2_), channel_id=1, source_target_pairs={{0,4},{1,3},{2,6},{3,1},{4,0},{5,7},{6,2},{7,5},{8,12},{9,11},{10,... | collective-permute-start | bytes 2359304 | tf_op jit(solution)/shard_map/ppermute | solution.py:383
  85.5 0.7 sum_my.1.refs_4_
  86.3 1.9 %collective-permute-start.13 = (bf16[768,512]{1,0:T(8,128)(2,1)S(1)}, bf16[768,512]{1,0:T(8,128)(2,1)S(1)}, u32[]{:S(2)}, u32[]{:S(2)}) collective-permute-start(bf16[768,512]{1,0:T(8,128)(2,1)S(1)} %sum_my.1.refs_4_), channel_id=1, source_target_pairs={{8,16},{16,8},{9,17},{17,9},{10,18},{18,10},{11,19},{19,11},{12,20... | collective-permute-start | bytes 2359304 | tf_op jit(solution)/shard_map/ppermute | solution.py:389
  88.2 1.0 sum_xh.1.refs_3_
  89.2 0.1 collective-permute-start.17
  89.3 11.1 %collective-permute-done.14.refs_2_ = bf16[768,512]{1,0:T(8,128)(2,1)S(1)} collective-permute-done((bf16[768,512]{1,0:T(8,128)(2,1)S(1)}, bf16[768,512]{1,0:T(8,128)(2,1)S(1)}, u32[]{:S(2)}, u32[]{:S(2)}) %collective-permute-start.14) | collective-permute-done | bytes 786464 | tf_op jit(solution)/shard_map/ppermute | solution.py:392
  100.4 1.5 %sum_f.1.refs_4_.refs_2_ = bf16[2,768,512]{2,1,0:T(8,128)(2,1)} custom-call(s32[23]{0:T(128)S(1)} %get-tuple-element.16.flags, bf16[2,768,512]{2,1,0:T(8,128)(2,1)S(1)} %get-tuple-element.25.refs_0_, bf16[768,512]{1,0:T(8,128)(2,1)S(1)} %collective-permute-done.12.refs_3_.refs_1_, bf16[768,512]{1,0:T(8,128)(2,1)S(1)} %collective-permute-done.14.refs_2_, ...), custom_call_target="tpu_custom_call" | custom-call | flops 1 | bytes 1 | tf_op jit(solution)/shard_map/sum_f/pallas_call | solution.py:359
  101.9 0.0 copy-start
  101.9 1.4 %copy-done = bf16[2,768,512]{2,1,0:T(8,128)(2,1)S(1)} copy-done((bf16[2,768,512]{2,1,0:T(8,128)(2,1)S(1)}, bf16[2,768,512]{2,1,0:T(8,128)(2,1)}, u32[]{:S(2)}) %copy-start) | copy-done | bytes 1572888
  103.3 1.0 sum_g0.1.refs_0_
  104.3 6.7 %collective-permute-done.17.refs_1_ = bf16[768,512]{1,0:T(8,128)(2,1)S(1)} collective-permute-done((bf16[768,512]{1,0:T(8,128)(2,1)S(1)}, bf16[768,512]{1,0:T(8,128)(2,1)S(1)}, u32[]{:S(2)}, u32[]{:S(2)}) %collective-permute-start.17) | collective-permute-done | bytes 786464 | tf_op jit(solution)/shard_map/ppermute | solution.py:392
  111.0 1.5 %finish.1 = bf16[2,768,512]{2,1,0:T(8,128)(2,1)} custom-call(s32[23]{0:T(128)S(1)} %get-tuple-element.16.flags, bf16[768,512]{1,0:T(8,128)(2,1)S(1)} %sum_g0.1.refs_0_, bf16[768,512]{1,0:T(8,128)(2,1)S(1)} %collective-permute-done.17.refs_1_, bf16[2,768,512]{2,1,0:T(8,128)(2,1)} %sum_f.1.refs_4_.refs_2_), custom_call_target="tpu_custom_call", output_to_operand_aliasing={{}: (3, {})} | custom-call | flops 1 | bytes 1 | tf_op jit(solution)/shard_map/finish/pallas_call | solution.py:359
  (9 shorter events, 0.0 us)
Async XLA Ops:
  4.8 12.2 %collective-permute-start.1 = (bf16[768,512]{1,0:T(8,128)(2,1)S(1)}, bf16[768,512]{1,0:T(8,128)(2,1)S(1)}, u32[]{:S(2)}, u32[]{:S(2)}) collective-permute-start(bf16[768,512]{1,0:T(8,128)(2,1)S(1)} %get-tuple-element.19.refs_0_), channel_id=1, source_target_pairs={{0,2},{1,5},{2,0},{3,7},{4,6},{5,1},{6,4},{7,3},{8,10},{9,13},{10,... | collective-permute-start | bytes 2359304 | tf_op jit(solution)/shard_map/ppermute | solution.py:383
  6.2 22.4 %collective-permute-start = (bf16[768,512]{1,0:T(8,128)(2,1)S(1)}, bf16[768,512]{1,0:T(8,128)(2,1)S(1)}, u32[]{:S(2)}, u32[]{:S(2)}) collective-permute-start(bf16[768,512]{1,0:T(8,128)(2,1)S(1)} %get-tuple-element.17.refs_0_), channel_id=1, source_target_pairs={{0,8},{24,16},{1,9},{25,17},{2,10},{26,18},{3,11},{27,19},{4,12},{... | collective-permute-start | bytes 2359304 | tf_op jit(solution)/shard_map/ppermute | solution.py:386
  16.4 21.4 %collective-permute-start.3 = (bf16[768,512]{1,0:T(8,128)(2,1)S(1)}, bf16[768,512]{1,0:T(8,128)(2,1)S(1)}, u32[]{:S(2)}, u32[]{:S(2)}) collective-permute-start(bf16[768,512]{1,0:T(8,128)(2,1)S(1)} %get-tuple-element.20.refs_2_.refs_0_), channel_id=1, source_target_pairs={{0,2},{1,5},{2,0},{3,7},{4,6},{5,1},{6,4},{7,3},{8,10},{9,13},{10,... | collective-permute-start | bytes 2359304 | tf_op jit(solution)/shard_map/ppermute | solution.py:383
  17.8 24.0 %collective-permute-start.7 = (bf16[768,512]{1,0:T(8,128)(2,1)S(1)}, bf16[768,512]{1,0:T(8,128)(2,1)S(1)}, u32[]{:S(2)}, u32[]{:S(2)}) collective-permute-start(bf16[768,512]{1,0:T(8,128)(2,1)S(1)} %sum_s3.1.refs_2_), channel_id=1, source_target_pairs={{0,4},{1,3},{2,6},{3,1},{4,0},{5,7},{6,2},{7,5},{8,12},{9,11},{10,... | collective-permute-start | bytes 2359304 | tf_op jit(solution)/shard_map/ppermute | solution.py:383
  21.2 24.2 %collective-permute-start.6 = (bf16[768,512]{1,0:T(8,128)(2,1)S(1)}, bf16[768,512]{1,0:T(8,128)(2,1)S(1)}, u32[]{:S(2)}, u32[]{:S(2)}) collective-permute-start(bf16[768,512]{1,0:T(8,128)(2,1)S(1)} %get-tuple-element.18.refs_0_), channel_id=1, source_target_pairs={{0,8},{24,16},{1,9},{25,17},{2,10},{26,18},{3,11},{27,19},{4,12},{... | collective-permute-start | bytes 2359304 | tf_op jit(solution)/shard_map/ppermute | solution.py:386
  29.3 17.8 %collective-permute-start.5 = (bf16[768,512]{1,0:T(8,128)(2,1)S(1)}, bf16[768,512]{1,0:T(8,128)(2,1)S(1)}, u32[]{:S(2)}, u32[]{:S(2)}) collective-permute-start(bf16[768,512]{1,0:T(8,128)(2,1)S(1)} %sum_ma.1.refs_0_), channel_id=1, source_target_pairs={{8,16},{16,8},{9,17},{17,9},{10,18},{18,10},{11,19},{19,11},{12,20... | collective-permute-start | bytes 2359304 | tf_op jit(solution)/shard_map/ppermute | solution.py:389
  38.7 21.5 %collective-permute-start.4 = (bf16[768,512]{1,0:T(8,128)(2,1)S(1)}, bf16[768,512]{1,0:T(8,128)(2,1)S(1)}, u32[]{:S(2)}, u32[]{:S(2)}) collective-permute-start(bf16[768,512]{1,0:T(8,128)(2,1)S(1)} %sum_s2.1.refs_3_), channel_id=1, source_target_pairs={{0,4},{1,3},{2,6},{3,1},{4,0},{5,7},{6,2},{7,5},{8,12},{9,11},{10,... | collective-permute-start | bytes 2359304 | tf_op jit(solution)/shard_map/ppermute | solution.py:383
  41.8 20.6 %collective-permute-start.9 = (bf16[768,512]{1,0:T(8,128)(2,1)S(1)}, bf16[768,512]{1,0:T(8,128)(2,1)S(1)}, u32[]{:S(2)}, u32[]{:S(2)}) collective-permute-start(bf16[768,512]{1,0:T(8,128)(2,1)S(1)} %get-tuple-element.26.refs_0_), channel_id=1, source_target_pairs={{0,2},{1,5},{2,0},{3,7},{4,6},{5,1},{6,4},{7,3},{8,10},{9,13},{10,... | collective-permute-start | bytes 2359304 | tf_op jit(solution)/shard_map/ppermute | solution.py:383
  42.7 22.7 %collective-permute-start.8 = (bf16[768,512]{1,0:T(8,128)(2,1)S(1)}, bf16[768,512]{1,0:T(8,128)(2,1)S(1)}, u32[]{:S(2)}, u32[]{:S(2)}) collective-permute-start(bf16[768,512]{1,0:T(8,128)(2,1)S(1)} %sum_g3.1.refs_2_.refs_0_), channel_id=1, source_target_pairs={{0,8},{24,16},{1,9},{25,17},{2,10},{26,18},{3,11},{27,19},{4,12},{... | collective-permute-start | bytes 2359304 | tf_op jit(solution)/shard_map/ppermute | solution.py:386
  45.5 25.1 %collective-permute-start.2 = (bf16[768,512]{1,0:T(8,128)(2,1)S(1)}, bf16[768,512]{1,0:T(8,128)(2,1)S(1)}, u32[]{:S(2)}, u32[]{:S(2)}) collective-permute-start(bf16[768,512]{1,0:T(8,128)(2,1)S(1)} %get-tuple-element.22.refs_0_), channel_id=1, source_target_pairs={{0,2},{1,5},{2,0},{3,7},{4,6},{5,1},{6,4},{7,3},{8,10},{9,13},{10,... | collective-permute-start | bytes 2359304 | tf_op jit(solution)/shard_map/ppermute | solution.py:383
  47.1 38.4 %collective-permute-start.12 = (bf16[768,512]{1,0:T(8,128)(2,1)S(1)}, bf16[768,512]{1,0:T(8,128)(2,1)S(1)}, u32[]{:S(2)}, u32[]{:S(2)}) collective-permute-start(bf16[768,512]{1,0:T(8,128)(2,1)S(1)} %sum_mb.1.refs_2_), channel_id=1, source_target_pairs={{8,16},{16,8},{9,17},{17,9},{10,18},{18,10},{11,19},{19,11},{12,20... | collective-permute-start | bytes 2359304 | tf_op jit(solution)/shard_map/ppermute | solution.py:389
  61.1 22.4 %collective-permute-start.11 = (bf16[768,512]{1,0:T(8,128)(2,1)S(1)}, bf16[768,512]{1,0:T(8,128)(2,1)S(1)}, u32[]{:S(2)}, u32[]{:S(2)}) collective-permute-start(bf16[768,512]{1,0:T(8,128)(2,1)S(1)} %sum_g2.1.refs_2_.refs_0_), channel_id=1, source_target_pairs={{0,8},{24,16},{1,9},{25,17},{2,10},{26,18},{3,11},{27,19},{4,12},{... | collective-permute-start | bytes 2359304 | tf_op jit(solution)/shard_map/ppermute | solution.py:386
  63.3 24.9 %collective-permute-start.15 = (bf16[768,512]{1,0:T(8,128)(2,1)S(1)}, bf16[768,512]{1,0:T(8,128)(2,1)S(1)}, u32[]{:S(2)}, u32[]{:S(2)}) collective-permute-start(bf16[768,512]{1,0:T(8,128)(2,1)S(1)} %sum_s1.1.refs_2_), channel_id=1, source_target_pairs={{0,4},{1,3},{2,6},{3,1},{4,0},{5,7},{6,2},{7,5},{8,12},{9,11},{10,... | collective-permute-start | bytes 2359304 | tf_op jit(solution)/shard_map/ppermute | solution.py:383
  66.1 22.1 %collective-permute-start.16 = (bf16[768,512]{1,0:T(8,128)(2,1)S(1)}, bf16[768,512]{1,0:T(8,128)(2,1)S(1)}, u32[]{:S(2)}, u32[]{:S(2)}) collective-permute-start(bf16[768,512]{1,0:T(8,128)(2,1)S(1)} %sum_mx.1.refs_2_), channel_id=1, source_target_pairs={{8,16},{16,8},{9,17},{17,9},{10,18},{18,10},{11,19},{19,11},{12,20... | collective-permute-start | bytes 2359304 | tf_op jit(solution)/shard_map/ppermute | solution.py:389
  70.6 29.8 %collective-permute-start.14 = (bf16[768,512]{1,0:T(8,128)(2,1)S(1)}, bf16[768,512]{1,0:T(8,128)(2,1)S(1)}, u32[]{:S(2)}, u32[]{:S(2)}) collective-permute-start(bf16[768,512]{1,0:T(8,128)(2,1)S(1)} %sum_xc.1.refs_3_), channel_id=1, source_target_pairs={{0,8},{8,0},{16,24},{24,16},{1,9},{9,1},{17,25},{25,17},{2,10},{10... | collective-permute-start | bytes 2359304 | tf_op jit(solution)/shard_map/ppermute | solution.py:392
  83.5 18.4 %collective-permute-start.10 = (bf16[768,512]{1,0:T(8,128)(2,1)S(1)}, bf16[768,512]{1,0:T(8,128)(2,1)S(1)}, u32[]{:S(2)}, u32[]{:S(2)}) collective-permute-start(bf16[768,512]{1,0:T(8,128)(2,1)S(1)} %sum_s0.1.refs_2_), channel_id=1, source_target_pairs={{0,4},{1,3},{2,6},{3,1},{4,0},{5,7},{6,2},{7,5},{8,12},{9,11},{10,... | collective-permute-start | bytes 2359304 | tf_op jit(solution)/shard_map/ppermute | solution.py:383
  86.3 15.6 %collective-permute-start.13 = (bf16[768,512]{1,0:T(8,128)(2,1)S(1)}, bf16[768,512]{1,0:T(8,128)(2,1)S(1)}, u32[]{:S(2)}, u32[]{:S(2)}) collective-permute-start(bf16[768,512]{1,0:T(8,128)(2,1)S(1)} %sum_my.1.refs_4_), channel_id=1, source_target_pairs={{8,16},{16,8},{9,17},{17,9},{10,18},{18,10},{11,19},{19,11},{12,20... | collective-permute-start | bytes 2359304 | tf_op jit(solution)/shard_map/ppermute | solution.py:389
  89.2 21.8 %collective-permute-start.17 = (bf16[768,512]{1,0:T(8,128)(2,1)S(1)}, bf16[768,512]{1,0:T(8,128)(2,1)S(1)}, u32[]{:S(2)}, u32[]{:S(2)}) collective-permute-start(bf16[768,512]{1,0:T(8,128)(2,1)S(1)} %sum_xh.1.refs_3_), channel_id=1, source_target_pairs={{0,8},{8,0},{16,24},{24,16},{1,9},{9,1},{17,25},{25,17},{2,10},{10... | collective-permute-start | bytes 2359304 | tf_op jit(solution)/shard_map/ppermute | solution.py:392
  101.9 1.4 %copy-start = (bf16[2,768,512]{2,1,0:T(8,128)(2,1)S(1)}, bf16[2,768,512]{2,1,0:T(8,128)(2,1)}, u32[]{:S(2)}) copy-start(bf16[2,768,512]{2,1,0:T(8,128)(2,1)} %sum_f.1.refs_4_.refs_2_) | copy-start | bytes 4718596
